TPU v7x, 256 devices: a whole 4x4x8 slice. The times are simulated.
256 devices in a mesh: pool: 32 (over z, x_lo, core), head: 8 (over y, x_hi).
Axes of the slice: x: 4 (x_hi: 2, x_lo: 2; x = x_hi * 2 + x_lo), y: 4, z: 8, core: 2. Of those that a mesh axis runs over, the one named last changes fastest.
Arguments:
- span_cache: bfloat16 [1024, 64, 576], P('pool'), may hold values from -6 to 6
- destination: int32 [1024, 1], P('pool'), may hold values from 0 to 31, as said below
- resident: bfloat16 [1536, 64, 576], P('pool'), may hold values from -6 to 6
- block_table: int32 [512, 32], P('pool'), may hold values from 0 to 111
- lengths: int32 [512], P('pool'), may hold values from 1 to 2048, as said below
- new_latent: bfloat16 [512, 4, 576], P('pool')
- query: bfloat16 [512, 4, 128, 192], P('pool', None, 'head')
- w_uk: bfloat16 [128, 128, 512], P('head'), may hold values from -0.5 to 0.5
- w_uv: bfloat16 [128, 512, 128], P('head'), may hold values from -0.25 to 0.25
- w_out: bfloat16 [16384, 7168], P('head', 'pool'), may hold values from -0.046875 to 0.046875
Outputs:
- layer_out: bfloat16 [512, 4, 7168], P('head', None, 'pool')
Inputs may be any that keep to these rules, and one draw needn't show every extreme that they name: Among the 32 blocks of one source, every destination that is named is named exactly 2 times. Every row's first lengths // 64 table entries and the partial one are read; some row has the largest length in every draw.
All inputs are finite; a program needn't handle non-finite values.
Results may differ from a plain program's by a relative error of at most 0.0076.
Values may be sent and summed in bfloat16 or wider, within the bound.
A program may use at most 192 MiB of HBM per device.

v0:
```python
import jax
import jax.numpy as jnp
from jax import lax
from jax.sharding import PartitionSpec as P


def per_device(
    span_cache, destination, resident, block_table, lengths, new_latent, query, w_uk, w_uv, w_out
):
    pool_n = lax.axis_size("pool")
    blocks, block_len, lat_width = span_cache.shape
    send_most = max(2, 2 * blocks // pool_n)
    dest_dev = destination[:, 0]
    onehot = (dest_dev[:, None] == jnp.arange(pool_n, dtype=jnp.int32)[None, :]).astype(jnp.int32)
    arrival_rank = jnp.sum((jnp.cumsum(onehot, axis=0) - onehot) * onehot, axis=1)
    target = dest_dev * send_most + arrival_rank
    placing = (target[None, :] == jnp.arange(pool_n * send_most, dtype=jnp.int32)[:, None]).astype(
        jnp.bfloat16
    )
    packed = jnp.einsum(
        "sb,btc->stc", placing, span_cache, preferred_element_type=jnp.float32
    ).astype(jnp.bfloat16)
    arrived = lax.all_to_all(packed, "pool", split_axis=0, concat_axis=0, tiled=True)
    page_pool = jnp.concatenate([resident, arrived], axis=0)
    rows_dev, steps, head_dev, qk_width = query.shape
    nope_width = w_uk.shape[1]
    latent_rank = w_uk.shape[2]
    softmax_scale = qk_width ** (-0.5)
    cached = page_pool[block_table].reshape(rows_dev, -1, lat_width)
    positions = jnp.arange(cached.shape[1], dtype=jnp.int32)
    causal = jnp.arange(steps)[:, None] >= jnp.arange(steps)[None, :]
    absorbed = jnp.einsum(
        "rthn,hnc->rthc", query[:, :, :, :nope_width], w_uk, preferred_element_type=jnp.float32
    ).astype(jnp.bfloat16)
    query_full = jnp.concatenate([absorbed, query[:, :, :, nope_width:]], axis=-1)
    old_scores = (
        jnp.einsum("rthc,rlc->rthl", query_full, cached, preferred_element_type=jnp.float32)
        * softmax_scale
    )
    old_scores = jnp.where(
        positions[None, None, None, :] < lengths[:, None, None, None], old_scores, -jnp.inf
    )
    new_scores = (
        jnp.einsum("rthc,rsc->rths", query_full, new_latent, preferred_element_type=jnp.float32)
        * softmax_scale
    )
    new_scores = jnp.where(causal[None, :, None, :], new_scores, -jnp.inf)
    highest = jnp.maximum(jnp.max(old_scores, axis=-1), jnp.max(new_scores, axis=-1))[..., None]
    old_exp = jnp.exp(old_scores - highest)
    new_exp = jnp.exp(new_scores - highest)
    denominator = jnp.sum(old_exp, axis=-1, keepdims=True) + jnp.sum(
        new_exp, axis=-1, keepdims=True
    )
    old_weights = (old_exp / denominator).astype(jnp.bfloat16)
    new_weights = (new_exp / denominator).astype(jnp.bfloat16)
    latent_mix = jnp.einsum(
        "rthl,rlc->rthc",
        old_weights,
        cached[:, :, :latent_rank],
        preferred_element_type=jnp.float32,
    )
    latent_mix = latent_mix + jnp.einsum(
        "rths,rsc->rthc",
        new_weights,
        new_latent[:, :, :latent_rank],
        preferred_element_type=jnp.float32,
    )
    latent_mix = latent_mix.astype(jnp.bfloat16)
    heads_out = jnp.einsum(
        "rthc,hcv->rthv", latent_mix, w_uv, preferred_element_type=jnp.float32
    ).astype(jnp.bfloat16)
    heads_out = heads_out.reshape(rows_dev, steps, -1)
    partial_value = jnp.einsum(
        "rtk,kd->rtd",
        lax.all_gather(heads_out, "pool", axis=0, tiled=True),
        w_out,
        preferred_element_type=jnp.float32,
    )
    return lax.psum_scatter(partial_value, "head", scatter_dimension=0, tiled=True).astype(
        jnp.bfloat16
    )


def solution(mesh):
    return jax.shard_map(
        per_device,
        mesh=mesh,
        in_specs=(
            P("pool", None, None),
            P("pool", None),
            P("pool", None, None),
            P("pool", None),
            P("pool"),
            P("pool", None, None),
            P("pool", None, "head", None),
            P("head", None, None),
            P("head", None, None),
            P("head", "pool"),
        ),
        out_specs=P("head", None, "pool"),
        check_vma=False,
    )
```

profile of v0, /device:TPU:17, one launch (start us, length us, event | category | flops | bytes accessed | tf_op | source)
XLA Modules:
  0.0 382.1 jit_solution(1372233373297685741)
XLA Ops:
  6.5 0.0 copy-start
  6.5 0.9 fusion.46
  7.4 0.1 reduce_window_sum.11
  7.5 0.8 select_reduce_fusion
  8.3 0.7 multiply_add_fusion
  9.0 0.0 copy-done
  9.0 2.8 convolution_convert_fusion
  11.8 5.4 %copy.31 = bf16[64,64,576]{2,1,0:T(8,128)(2,1)} copy(bf16[64,64,576]{2,0,1:T(8,128)(2,1)S(1)} %convolution_convert_fusion) | data formatting | bytes 9437184 | tf_op jit(solution)/shard_map/convert_element_type | solution.py:22
  17.1 0.0 copy-start.5
  17.1 0.0 slice-start.1
  17.2 10.4 %all-to-all-start = ((bf16[64,64,576]{2,1,0:T(8,128)(2,1)}), bf16[64,64,576]{2,1,0:T(8,128)(2,1)}, u32[]{:S(2)}, u32[]{:S(2)}) async-start(bf16[64,64,576]{2,1,0:T(8,128)(2,1)} %copy.31), calls=%async_computation | async-start | bytes 10485760 | tf_op jit(solution)/shard_map/all_to_all | solution.py:23
  27.6 0.0 copy-start.4
  27.6 0.0 copy-start.6
  27.6 0.0 all-gather.2.cloned.1.call-start
  27.6 0.0 copy-done.5
  27.7 0.1 reshape.62
  27.7 0.0 slice-done.1
  27.7 0.2 copy.47
  27.9 0.0 slice-done
  28.0 2.0 fusion.16
  30.0 0.1 pad_maximum_fusion.1
  30.1 0.0 copy-done.4
  30.2 2.0 fusion.52
  32.2 0.0 copy-done.6
  32.2 0.1 iota_compare_fusion
  32.3 114.4 %all-to-all-done = bf16[64,64,576]{2,1,0:T(8,128)(2,1)} async-done(((bf16[64,64,576]{2,1,0:T(8,128)(2,1)}), bf16[64,64,576]{2,1,0:T(8,128)(2,1)}, u32[]{:S(2)}, u32[]{:S(2)}) %all-to-all-start) | async-done | bytes 4718624 | tf_op jit(solution)/shard_map/all_to_all | solution.py:23
  146.6 8.4 %pad_maximum_fusion = bf16[112,64,576]{2,1,0:T(8,128)(2,1)} fusion(bf16[64,64,576]{2,1,0:T(8,128)(2,1)} %all-to-all-done, bf16[48,64,576]{2,1,0:T(8,128)(2,1)} %param.12), kind=kLoop, calls=%fused_computation.3 | loop fusion | flops 4128768 | bytes 16515072 | tf_op jit(solution)/shard_map/concatenate | solution.py:24
  155.0 22.9 %gather_fusion = bf16[512,64,576]{2,1,0:T(8,128)(2,1)} fusion(bf16[112,64,576]{2,1,0:T(8,128)(2,1)} %pad_maximum_fusion, s32[1024]{0:T(1024)S(1)} %pad_clamp_fusion), kind=kCustom, calls=%fused_computation | custom fusion | bytes 75499520 | tf_op jit(solution)/shard_map/gather | solution.py:29
  177.9 20.9 %fusion.1 = (f32[16,4,16]{2,1,0:T(4,128)S(1)}, f32[16,4,16,2048]{3,2,1,0:T(8,128)}) fusion(pred[16,2048]{1,0:T(8,128)(4,1)S(1)} %iota_compare_fusion, bf16[16,2048,576,1]{2,1,3,0:T(8,128)(2,1)} %bitcast.60, bf16[16,4,16,576]{3,0,1,2:T(8,128)(2,1)S(1)} %pad_maximum_fusion.1), kind=kOutput, calls=%fused_computation.7 | convolution fusion | flops 2422209536 | bytes 47353856 | tf_op jit(solution)/shard_map/rthc,rlc->rthl/dot_general | solution.py:37
  198.9 0.1 fusion.39
  199.0 5.1 %fusion.2 = f32[16,4,16]{2,1,0:T(4,128)S(1)} fusion(f32[16,4,16,2048]{3,2,1,0:T(8,128)} %get-tuple-element.6, f32[16,4,16]{2,1,0:T(4,128)S(1)} %max.7, pred[16,2048]{1,0:T(8,128)(4,1)S(1)} %iota_compare_fusion), kind=kLoop, calls=%fused_computation.8 | loop fusion | flops 8387584 | bytes 8429568 | tf_op jit(solution)/shard_map/reduce_sum | solution.py:51
  204.2 0.5 fusion.41
  204.7 0.2 copy-done.2
  204.9 13.5 %add_convert_fusion = bf16[16,4,16,512]{3,2,1,0:T(8,128)(2,1)S(1)} fusion(f32[16,4,16,512]{3,2,1,0:T(8,128)S(1)} %fusion.41, bf16[16,2048,576]{2,1,0:T(8,128)(2,1)} %bitcast.61, f32[16,4,16,2048]{3,2,1,0:T(8,128)S(1)} %copy-done.2, f32[16,4,16]{2,1,0:T(4,128)S(1)} %add.29, f32[16,4,16]{2,1,0:T(4,128)S(1)} %max.7, pred[16,2048]{1,0:T(8,128)(4,1)S(1)} %iota_compare_fusion), kind=kOutput, calls=%fused_computation.20 | convolution fusion | flops 2159017984 | bytes 45129728 | tf_op jit(solution)/shard_map/rthl,rlc->rthc/dot_general | solution.py:56
  218.4 0.0 copy-done.3
  218.4 1.4 fusion.22
  219.8 0.8 copy.68
  220.6 0.0 all-gather.2.cloned.1.call-update
  220.6 0.0 copy-start.1
  220.6 0.0 reduce-scatter.2.cloned.1.call-start
  220.6 68.6 %all-gather.2.cloned.1.call-done = bf16[512,4,2048]{2,0,1:T(8,128)(2,1)} async-done(((bf16[16,4,2048]{2,0,1:T(8,128)(2,1)}), bf16[512,4,2048]{2,0,1:T(8,128)(2,1)}) %all-gather.2.cloned.1.call-update) | async-done | bytes 8388624 | tf_op jit(solution)/shard_map/all_gather | solution.py:75
  289.3 0.0 copy-done.7
  289.3 7.1 %fusion.36 = f32[512,4,224]{2,0,1:T(8,128)} fusion(bf16[512,4,2048]{2,0,1:T(8,128)(2,1)} %all-gather.2.cloned.1.call-done, bf16[2048,224]{0,1:T(8,128)(2,1)S(1)} %copy-done.7), kind=kOutput, calls=%fused_computation.33 | convolution fusion | flops 1879048192 | bytes 11141120 | tf_op jit(solution)/shard_map/rtk,kd->rtd/dot_general | solution.py:73
  296.4 0.0 reduce-scatter.2.cloned.1.call-update
  296.4 77.1 %reduce-scatter.2.cloned.1.call-done = f32[64,4,224]{2,0,1:T(8,128)} async-done(((f32[512,4,224]{2,0,1:T(8,128)}), f32[64,4,224]{2,0,1:T(8,128)}) %reduce-scatter.2.cloned.1.call-update) | async-done | bytes 229392 | tf_op jit(solution)/shard_map/reduce_scatter | solution.py:79
  373.5 1.0 convert_element_type.40
  374.5 0.8 copy.37
  375.2 0.0 copy-done.1
  (9 shorter events, 0.0 us)
Async XLA Ops:
  6.5 2.4 copy-start
  17.1 10.5 %copy-start.5 = (s32[16,32]{1,0:T(8,128)S(1)}, s32[16,32]{1,0:T(8,128)}, u32[]{:S(2)}) copy-start(s32[16,32]{1,0:T(8,128)} %param.13) | copy-start | bytes 6148
  17.1 10.6 %slice-start.1 = ((bf16[16,4,16,192]{3,2,1,0:T(8,128)(2,1)}), bf16[16,4,16,64]{3,2,1,0:T(8,128)(2,1)S(1)}, s32[]{:S(2)}) async-start(bf16[16,4,16,192]{3,2,1,0:T(8,128)(2,1)} %param.16), calls=%async_computation.5 | async-start | bytes 524288 | tf_op jit(solution)/shard_map/slice | solution.py:35
  17.2 10.8 %slice-start = ((bf16[16,4,16,192]{3,2,1,0:T(8,128)(2,1)}), bf16[16,4,16,128]{3,2,1,0:T(8,128)(2,1)S(1)}, s32[]{:S(2)}) async-start(bf16[16,4,16,192]{3,2,1,0:T(8,128)(2,1)} %param.16), calls=%async_computation.4 | async-start | bytes 524288 | tf_op jit(solution)/shard_map/slice | solution.py:33
  17.2 129.5 %all-to-all-start = ((bf16[64,64,576]{2,1,0:T(8,128)(2,1)}), bf16[64,64,576]{2,1,0:T(8,128)(2,1)}, u32[]{:S(2)}, u32[]{:S(2)}) async-start(bf16[64,64,576]{2,1,0:T(8,128)(2,1)} %copy.31), calls=%async_computation | async-start | bytes 10485760 | tf_op jit(solution)/shard_map/all_to_all | solution.py:23
  27.6 2.6 copy-start.4
  27.6 4.6 %copy-start.6 = (s32[16]{0:T(128)S(1)}, s32[16]{0:T(128)}, u32[]{:S(2)}) copy-start(s32[16]{0:T(128)} %param.14) | copy-start | bytes 196
  27.6 261.7 %all-gather.2.cloned.1.call-start = ((), (), s32[]{:S(2)}) async-start(), calls=%async_computation.2 | async-start | bytes 8650752 | tf_op jit(solution)/shard_map/all_gather | solution.py:75
  199.0 5.8 %copy-start.2 = (f32[16,4,16,2048]{3,2,1,0:T(8,128)S(1)}, f32[16,4,16,2048]{3,2,1,0:T(8,128)}, u32[]{:S(2)}) copy-start(f32[16,4,16,2048]{3,2,1,0:T(8,128)} %get-tuple-element.6) | copy-start | bytes 25165828
  204.9 13.5 %copy-start.3 = (bf16[16,512,128]{2,1,0:T(8,128)(2,1)S(1)}, bf16[16,512,128]{2,1,0:T(8,128)(2,1)}, u32[]{:S(2)}) copy-start(bf16[16,512,128]{2,1,0:T(8,128)(2,1)} %param.18) | copy-start | bytes 6291460
  204.9 84.4 %copy-start.7 = (bf16[2048,224]{0,1:T(8,128)(2,1)S(1)}, bf16[2048,224]{0,1:T(8,128)(2,1)}, u32[]{:S(2)}) copy-start(bf16[2048,224]{0,1:T(8,128)(2,1)} %param.19) | copy-start | bytes 2752516
  220.6 154.7 %copy-start.1 = (bf16[32,64,576]{2,1,0:T(8,128)(2,1)S(1)}, bf16[32,64,576]{2,1,0:T(8,128)(2,1)}, u32[]{:S(2)}) copy-start(bf16[32,64,576]{2,1,0:T(8,128)(2,1)} %param.10) | copy-start | bytes 7077892
  220.6 152.9 %reduce-scatter.2.cloned.1.call-start = ((), (), s32[]{:S(2)}) async-start(), calls=%async_computation.3 | async-start | bytes 2359296 | tf_op jit(solution)/shard_map/reduce_scatter | solution.py:79
Sparse Core Ops, SparseCore 0:
  220.7 68.5 all-gather.1
  296.6 76.9 reduce-scatter.1
where the time goes:
time: 385 us; the launch traced here: 382 us
  waiting for transfers between devices  260 us (68%)
  matrix products  50.3 us (13%)
  local copies, waits for them, and re-layouts  30.3 us (8%)
  other arithmetic  17.3 us (4%)
  between operations  13.6 us (4%)
  starting transfers between devices  10.5 us (3%)
    all_to_all x1, waiting for transfers between devices, per_device(): lax.all_to_all(packed, 'pool', split_axis=0, concat_axis=0, tiled=True)  114 us
    reduce_scatter x1, waiting for transfers between devices, per_device(): lax.psum_scatter(partial_value, 'head', scatter_dimension=0, tiled=True)  77.1 us
    all_gather x1, waiting for transfers between devices, per_device(): lax.all_gather(heads_out, 'pool', axis=0, tiled=True)  68.6 us
    gather x1, local copies, waits for them, and re-layouts, per_device(): cached = page_pool[block_table].reshape(rows_dev, -1, lat_width)  22.9 us
    dot_general x1, matrix products, per_device(): jnp.einsum('rthc,rlc->rthl', query_full, cached, preferred_element_type=j...  20.9 us
    dot_general x1, matrix products, per_device(): jnp.einsum('rthl,rlc->rthc', old_weights, cached[:, :, :latent_rank], pre...  13.5 us
    all_to_all x1, starting transfers between devices, per_device(): lax.all_to_all(packed, 'pool', split_axis=0, concat_axis=0, tiled=True)  10.4 us
    concatenate x1, other arithmetic, per_device(): page_pool = jnp.concatenate([resident, arrived], axis=0)  8.41 us
  transfers between devices with their start and end apart: 3, of which 3 were waited for; matrix products, arithmetic and copies ran while one was open for 1% of the time, Pallas kernels for 0%

commit v1 on v0

v1 whole, which is shorter than its diff:
```python
import functools

import jax
import jax.numpy as jnp
from jax import lax
from jax.experimental import pallas as pl
from jax.experimental.pallas import tpu as pltpu
from jax.sharding import PartitionSpec as P

MESH = pl.DeviceIdType.MESH
F32 = jnp.float32
BF16 = jnp.bfloat16
NT = (((1,), (1,)), ((), ()))
NN = (((1,), (0,)), ((), ()))


def coords():
    p = lax.axis_index("pool")
    h = lax.axis_index("head")
    return p // 4, lax.rem(p // 2, 2), lax.rem(p, 2), h // 2, lax.rem(h, 2)


def peer_of(e, k, z, xl, c, y, sign):
    dz = lax.rem(y + k, 4) + 4 * e
    zz = lax.rem(z + 8 + sign * dz, 8)
    return zz * 4 + lax.rem(xl + k // 2, 2) * 2 + lax.rem(c + k % 2, 2)


def attend_kernel(
    pick, q3, bias, span, resident, fresh, w_uk, w_uv, w_out,
    heads_out, wall,
    span_v, res_v, uk_v, uv_v, fresh_v, sendbuf, arr, q_abs, acc, m_s, l_s, out_v,
    load_sem, res_sem, zsend, zrecv, ysend, yrecv, wsend, wrecv, out_sem,
):
    z, xl, c, y, xh = coords()
    p = lax.axis_index("pool")
    h = lax.axis_index("head")
    g = lax.rem(p, 4)
    up = lax.rem(y + 1, 4) * 2 + xh
    down = lax.rem(y + 3, 4) * 2 + xh
    core_mate = p + 1 - 2 * c
    xl_mate = p + 2 - 4 * xl
    pairs = [(e, k) for e in range(2) for k in range(4)]

    loads = [
        pltpu.make_async_copy(span, span_v, load_sem.at[0]),
        pltpu.make_async_copy(w_uk, uk_v, load_sem.at[1]),
        pltpu.make_async_copy(fresh, fresh_v, load_sem.at[2]),
        pltpu.make_async_copy(w_uv, uv_v, load_sem.at[3]),
    ]
    res_loads = [
        pltpu.make_async_copy(resident.at[pl.ds(512 * n, 512)], res_v.at[pl.ds(512 * n, 512)], res_sem.at[n])
        for n in range(6)
    ]
    for one in loads[:3] + res_loads + loads[3:]:
        one.start()

    barrier = pltpu.get_barrier_semaphore()

    def greet(pool_to, head_to):
        pl.semaphore_signal(barrier, inc=1, device_id=(pool_to, head_to), device_id_type=MESH)

    for e, k in pairs:
        for sign in (1, -1):
            to = peer_of(e, k, z, xl, c, y, sign)
            if (e, k) == (0, 0):
                @pl.when(y != 0)
                def _(to=to):
                    greet(to, h)
            else:
                greet(to, h)
    greet(p, up)
    greet(p, down)
    greet(core_mate, h)
    greet(xl_mate, h)
    pl.semaphore_wait(barrier, 18 + 2 * jnp.where(y != 0, 1, 0))

    loads[0].wait()
    zcopies = []
    for e, k in pairs:
        i = e * 4 + k
        for ab in range(2):
            at = pick[i, ab]
            live = pick[i, 2]
            block = span_v[at] * live.astype(F32).astype(BF16)
            for slab in range(4):
                sendbuf[i, ab * 4 + slab] = block[:, slab * 128 : (slab + 1) * 128]
            if ab == 0:
                low = block[:, 512:]
            else:
                sendbuf[i, 8] = jnp.concatenate([low, block[:, 512:]], axis=1)
        to = peer_of(e, k, z, xl, c, y, 1)
        remote = pltpu.make_async_remote_copy(
            src_ref=sendbuf.at[i], dst_ref=arr.at[0, e, :, k], send_sem=zsend.at[i], recv_sem=zrecv.at[i],
            device_id=(to, h), device_id_type=MESH,
        )
        zcopies.append(remote)
        if i == 0:
            @pl.when(y != 0)
            def _(remote=remote):
                remote.start()

            @pl.when(y == 0)
            def _():
                pltpu.make_async_copy(sendbuf.at[0], arr.at[0, 0, :, 0], zrecv.at[0]).start()
        else:
            remote.start()

    def wcopy(src, owner, to, n):
        slot = lax.rem(owner - lax.rem(to, 4) + 4, 4) - 1
        return pltpu.make_async_remote_copy(
            src_ref=src, dst_ref=wall.at[slot], send_sem=wsend.at[n], recv_sem=wrecv.at[n],
            device_id=(to, h), device_id_type=MESH,
        )

    w_mate = wcopy(w_out, g, core_mate, 0)
    w_far = wcopy(w_out, g, xl_mate, 1)
    w_pass = wcopy(wall.at[1], lax.rem(g + 2, 4), core_mate, 2)
    w_mate.start()
    w_far.start()

    loads[1].wait()

    @pl.loop(0, 16)
    def _(hd):
        at = pl.ds(pl.multiple_of(hd * 64, 64), 64)
        q_abs[at, :] = jnp.dot(q3[at, :128], uk_v[hd], preferred_element_type=F32).astype(BF16)

    scale = 1.4426950408889634 * 192 ** -0.5
    TQ = 256

    def fold(at, s, values, first=False):
        top = jnp.max(s, axis=1, keepdims=True)
        if not first:
            before = m_s[at, :1]
            top = jnp.maximum(top, before)
        p_ = jnp.exp2(s - top)
        total = jnp.sum(p_, axis=1, keepdims=True)
        mix = lax.dot_general(p_.astype(BF16), values, NN, preferred_element_type=F32)
        if not first:
            fade = jnp.exp2(before - top)
            total = total + l_s[at, :1] * fade
            mix = mix + acc[at, :] * fade
        acc[at, :] = mix
        m_s[at, :] = jnp.broadcast_to(top, (TQ, 128))
        l_s[at, :] = jnp.broadcast_to(total, (TQ, 128))

    def biased(s, row):
        return (s.reshape(TQ // 16, 16, s.shape[1]) * scale + row[None]).reshape(s.shape)

    loads[2].wait()

    @pl.loop(0, 1024 // TQ)
    def _(n):
        at = pl.ds(pl.multiple_of(n * TQ, TQ), TQ)
        s = lax.dot_general(q_abs[at, :], fresh_v[:, :512], NT, preferred_element_type=F32)
        s = s + lax.dot_general(q3[at, 128:192], fresh_v[:, 512:], NT, preferred_element_type=F32)
        row = lax.broadcasted_iota(jnp.int32, s.shape, 0)
        col = lax.broadcasted_iota(jnp.int32, s.shape, 1)
        seen = ((row & 15) == (col >> 2)) & (((row >> 4) & 3) >= (col & 3))
        fold(at, jnp.where(seen, s * scale, -jnp.inf), fresh_v[:, :512], first=True)

    def resident_chunk(n):
        res_loads[n].wait()
        toks = pl.ds(512 * n, 512)

        @pl.loop(0, 1024 // TQ)
        def _(t):
            at = pl.ds(pl.multiple_of(t * TQ, TQ), TQ)
            s = lax.dot_general(q_abs[at, :], res_v[toks, :512], NT, preferred_element_type=F32)
            s = s + lax.dot_general(q3[at, 128:192], res_v[toks, 512:], NT, preferred_element_type=F32)
            fold(at, biased(s, bias[:, toks]), res_v[toks, :512])

    def arrived_chunk(rel, e):
        n = rel * 2 + e

        @pl.loop(0, 1024 // TQ)
        def _(t):
            at = pl.ds(pl.multiple_of(t * TQ, TQ), TQ)
            rope = arr[rel, e, 8].reshape(256, 128)
            parts, mains = [], []
            for ab in range(2):
                main = jnp.concatenate([arr[rel, e, ab * 4 + j].reshape(256, 128) for j in range(4)], axis=1)
                s = lax.dot_general(q_abs[at, :], main, NT, preferred_element_type=F32)
                s = s + lax.dot_general(
                    q3[at, 128 * (1 + ab) : 128 * (2 + ab)], rope, NT, preferred_element_type=F32
                )
                parts.append(s)
                mains.append(main)
            s = jnp.concatenate(parts, axis=1)
            fold(at, biased(s, bias[:, 3072 + 512 * n : 3584 + 512 * n]), jnp.concatenate(mains, axis=0))

    def ycopy(i, way, kind):
        e, k = pairs[i]
        landing = 2 if kind else (3 if way == 0 else 1)
        source = 0 if kind == 0 else (3 if way == 0 else 1)
        return pltpu.make_async_remote_copy(
            src_ref=arr.at[source, e, :, k], dst_ref=arr.at[landing, e, :, k],
            send_sem=ysend.at[way, kind, i], recv_sem=yrecv.at[way, kind, i],
            device_id=(p, up if way == 0 else down), device_id_type=MESH,
        )

    def own_step(i):
        if i == 0:
            @pl.when(y != 0)
            def _():
                zcopies[0].wait_recv()

            @pl.when(y == 0)
            def _():
                pltpu.make_async_copy(sendbuf.at[0], arr.at[0, 0, :, 0], zrecv.at[0]).wait()
        else:
            zcopies[i].wait_recv()
        ycopy(i, 0, 0).start()
        ycopy(i, 1, 0).start()

    def pass_step(i):
        ycopy(i, 0, 0).wait_recv()
        ycopy(i, 1, 0).wait_recv()
        ycopy(i, i % 4 // 2, 1).start()

    for i in range(8):
        if i < 6:
            resident_chunk(i)
        own_step(i)
        if i > 0:
            pass_step(i - 1)
        if i == 3:
            w_far.wait_recv()
            w_pass.start()
        if i == 5:
            arrived_chunk(0, 0)
        if i == 6:
            arrived_chunk(3, 0)
            arrived_chunk(1, 0)
    arrived_chunk(0, 1)
    pass_step(7)
    arrived_chunk(3, 1)
    arrived_chunk(1, 1)
    for i in range(8):
        ycopy(i, i % 4 // 2, 1).wait_recv()
        if i == 3:
            arrived_chunk(2, 0)
    arrived_chunk(2, 1)

    loads[3].wait()

    @pl.loop(0, 4)
    def _(quarter):
        for j in range(4):
            hd = quarter * 4 + j
            at = pl.ds(pl.multiple_of(hd * 64, 64), 64)
            mixed = (acc[at, :] / l_s[at, :1]).astype(BF16)
            out_v[:, pl.ds(pl.multiple_of(hd * 128, 128), 128)] = jnp.dot(
                mixed, uv_v[hd], preferred_element_type=F32
            ).astype(BF16)

    done = pltpu.make_async_copy(out_v, heads_out, out_sem)
    done.start()

    @pl.when(y != 0)
    def _():
        zcopies[0].wait_send()

    for i in range(1, 8):
        zcopies[i].wait_send()
    for i in range(8):
        ycopy(i, 0, 0).wait_send()
        ycopy(i, 1, 0).wait_send()
        ycopy(i, i % 4 // 2, 1).wait_send()
    w_mate.wait()
    w_far.wait_send()
    w_pass.wait()
    done.wait()


def project_kernel(
    heads, w_out, wall,
    out,
    w_v, hbuf, tiles, landed, load_sem, zsend, zrecv, rsend, rrecv,
):
    p = lax.axis_index("pool")
    h = lax.axis_index("head")
    z, g = p // 4, lax.rem(p, 4)
    right = lax.rem(z + 1, 8) * 4 + g
    left = lax.rem(z + 7, 8) * 4 + g

    own = pltpu.make_async_copy(heads, hbuf.at[0], load_sem.at[4])
    own.start()
    w_loads = [pltpu.make_async_copy(w_out, w_v.at[0], load_sem.at[0])] + [
        pltpu.make_async_copy(wall.at[i], w_v.at[i + 1], load_sem.at[i + 1]) for i in range(3)
    ]
    for one in w_loads:
        one.start()

    barrier = pltpu.get_barrier_semaphore()

    def greet(pool_to, head_to):
        pl.semaphore_signal(barrier, inc=1, device_id=(pool_to, head_to), device_id_type=MESH)

    greet(right, h)
    greet(left, h)
    for dh in range(8):
        for i in range(4):
            if dh or i:
                greet(z * 4 + lax.rem(g + i, 4), lax.rem(h + dh, 8))
    pl.semaphore_wait(barrier, 33)

    def zcopy(way, a, half):
        rows = pl.ds(32 * half, 32)
        src = 0 if a == 1 else 2 * (a - 1) - 1 + way
        dst = 7 if a == 4 else 2 * a - 1 + way
        return pltpu.make_async_remote_copy(
            src_ref=hbuf.at[src, rows], dst_ref=hbuf.at[dst, rows],
            send_sem=zsend.at[way, a - 1, half], recv_sem=zrecv.at[way, a - 1, half],
            device_id=(right if way == 0 else left, h), device_id_type=MESH,
        )

    own.wait()
    order = [(0, 0), (0, 1), (1, 1), (1, 0)]
    for way, half in order:
        zcopy(way, 1, half).start()

    def tile_copy(slot, i, to_head):
        return pltpu.make_async_remote_copy(
            src_ref=tiles.at[slot, i], dst_ref=landed.at[h, g],
            send_sem=rsend.at[slot, i], recv_sem=rrecv.at[h, g],
            device_id=(z * 4 + lax.rem(g + i, 4), to_head), device_id_type=MESH,
        )

    def slot_head(slot):
        if slot == 0:
            return z
        if slot == 7:
            return lax.rem(z + 4, 8)
        a = (slot + 1) // 2
        return lax.rem(z + 8 - a, 8) if slot % 2 else lax.rem(z + a, 8)

    def multiply(first, count):
        lhs = hbuf[pl.ds(first, count)].reshape(64 * count, 2048)
        for i in range(4):
            part = jnp.dot(lhs, w_v[i], preferred_element_type=F32).astype(BF16)
            for n in range(count):
                slot = first + n
                to_head = slot_head(slot)
                tiles[slot, i] = part[64 * n : 64 * (n + 1)]
                copy = tile_copy(slot, i, to_head)
                if i == 0:
                    @pl.when(to_head != h)
                    def _(copy=copy):
                        copy.start()

                    @pl.when(to_head == h)
                    def _(slot=slot):
                        landed[h, g] = tiles[slot, 0]
                else:
                    copy.start()

    for one in w_loads:
        one.wait()
    multiply(0, 1)
    for a in range(1, 4):
        for way, half in order:
            zcopy(way, a, half).wait_recv()
            if a < 3 or way == half:
                zcopy(way, a + 1, half).start()
        multiply(2 * a - 1, 2)
    zcopy(0, 4, 0).wait_recv()
    zcopy(1, 4, 1).wait_recv()
    multiply(7, 1)

    for dh in range(8):
        for i in range(4):
            if dh or i:
                hh, gg = lax.rem(h + dh, 8), lax.rem(g + i, 4)
                pltpu.make_async_remote_copy(
                    src_ref=tiles.at[0, 0], dst_ref=landed.at[hh, gg],
                    send_sem=rsend.at[0, 0], recv_sem=rrecv.at[hh, gg],
                    device_id=(z * 4 + gg, hh), device_id_type=MESH,
                ).wait_recv()
    total = landed[0].astype(F32)
    for n in range(1, 8):
        total = total + landed[n].astype(F32)
    out[...] = total.astype(BF16)

    for way, half in order:
        for a in range(1, 5):
            if a < 4 or way == half:
                zcopy(way, a, half).wait_send()
    for slot in range(8):
        to_head = slot_head(slot)
        for i in range(4):
            if i == 0:
                @pl.when(to_head != h)
                def _(slot=slot, to_head=to_head):
                    tile_copy(slot, 0, to_head).wait_send()
            else:
                tile_copy(slot, i, to_head).wait_send()


ANY = pl.BlockSpec(memory_space=pl.ANY)
VMEM = pl.BlockSpec(memory_space=pltpu.VMEM)
SMEM = pl.BlockSpec(memory_space=pltpu.SMEM)
DMA = pltpu.SemaphoreType.DMA


def attend(span_cache, destination, resident, block_table, lengths, new_latent, query, w_uk, w_uv, w_out):
    z, xl, c, y, xh = coords()
    owners = jnp.stack([peer_of(e, k, z, xl, c, y, 1) for e in range(2) for k in range(4)])
    named = destination[:, 0][None, :] == owners[:, None]
    at = lax.broadcasted_iota(jnp.int32, named.shape, 1)
    last = jnp.max(jnp.where(named, at, 0), axis=1)
    first = 31 - jnp.max(jnp.where(named, 31 - at, 0), axis=1)
    pick = jnp.stack([first, last, jnp.any(named, axis=1).astype(jnp.int32)], axis=1)

    rel, e, ab, k = (lax.broadcasted_iota(jnp.int32, (4, 2, 2, 4), d) for d in range(4))
    dz = lax.rem(y + rel + k, 4) + 4 * e
    source = lax.rem(z + 8 - dz, 8) * 4 + lax.rem(xl + k // 2, 2) * 2 + lax.rem(c + k, 2)
    pages = jnp.concatenate([jnp.arange(48, dtype=jnp.int32), (48 + source * 2 + ab).reshape(-1)])
    hit = block_table[:, :, None] == pages[None, None, :]
    col = jnp.arange(32, dtype=jnp.int32)[None, :, None]
    full = (lengths // 64)[:, None, None]
    count = jnp.sum((hit & (col < full)).astype(jnp.int32), axis=1)
    partial = jnp.sum((hit & (col == full)).astype(jnp.int32), axis=1)
    inside = jnp.arange(64, dtype=jnp.int32)[None, None, :] < lax.rem(lengths, 64)[:, None, None]
    reads = count[:, :, None] + partial[:, :, None] * inside.astype(jnp.int32)
    bias = jnp.log2(reads.astype(F32)).reshape(16, 112 * 64)

    q = query.transpose(2, 1, 0, 3).reshape(1024, 192)
    none = jnp.zeros((1024, 64), BF16)
    q3 = jnp.concatenate([q, none, none, q[:, 128:]], axis=1)

    return pl.pallas_call(
        attend_kernel,
        out_shape=(
            jax.ShapeDtypeStruct((64, 2048), BF16),
            jax.ShapeDtypeStruct((3, 2048, 224), BF16),
        ),
        in_specs=[SMEM, VMEM, VMEM, ANY, ANY, ANY, ANY, ANY, ANY],
        out_specs=(ANY, ANY),
        scratch_shapes=[
            pltpu.VMEM((32, 64, 576), BF16),
            pltpu.VMEM((3072, 576), BF16),
            pltpu.VMEM((16, 128, 512), BF16),
            pltpu.VMEM((16, 512, 128), BF16),
            pltpu.VMEM((64, 576), BF16),
            pltpu.VMEM((8, 9, 64, 128), BF16),
            pltpu.VMEM((4, 2, 9, 4, 64, 128), BF16),
            pltpu.VMEM((1024, 512), BF16),
            pltpu.VMEM((1024, 512), F32),
            pltpu.VMEM((1024, 128), F32),
            pltpu.VMEM((1024, 128), F32),
            pltpu.VMEM((64, 2048), BF16),
            DMA((4,)), DMA((6,)), DMA((8,)), DMA((8,)),
            DMA((2, 2, 8)), DMA((2, 2, 8)), DMA((3,)), DMA((3,)), DMA,
        ],
        compiler_params=pltpu.CompilerParams(
            collective_id=0, has_side_effects=True, vmem_limit_bytes=56 * 1024 * 1024
        ),
        name="handoff_attend",
    )(pick, q3, bias, span_cache, resident.reshape(3072, 576), new_latent.reshape(64, 576), w_uk, w_uv, w_out)


def project(heads, w_out, wall):
    out = pl.pallas_call(
        project_kernel,
        out_shape=jax.ShapeDtypeStruct((4, 64, 224), BF16),
        in_specs=[ANY, ANY, ANY],
        out_specs=VMEM,
        scratch_shapes=[
            pltpu.VMEM((4, 2048, 224), BF16),
            pltpu.VMEM((8, 64, 2048), BF16),
            pltpu.VMEM((8, 4, 64, 224), BF16),
            pltpu.VMEM((8, 4, 64, 224), BF16),
            DMA((5,)), DMA((2, 4, 2)), DMA((2, 4, 2)), DMA((8, 4)), DMA((8, 4)),
        ],
        compiler_params=pltpu.CompilerParams(
            collective_id=1, has_side_effects=True, vmem_limit_bytes=56 * 1024 * 1024
        ),
        name="gather_project",
    )(heads, w_out, wall)
    return out.reshape(4, 4, 16, 224).transpose(0, 2, 1, 3).reshape(64, 4, 224)


def per_device(
    span_cache, destination, resident, block_table, lengths, new_latent, query, w_uk, w_uv, w_out
):
    heads, wall = attend(
        span_cache, destination, resident, block_table, lengths, new_latent, query, w_uk, w_uv, w_out
    )
    return project(heads, w_out, wall)


def solution(mesh):
    return jax.shard_map(
        per_device,
        mesh=mesh,
        in_specs=(
            P("pool", None, None),
            P("pool", None),
            P("pool", None, None),
            P("pool", None),
            P("pool"),
            P("pool", None, None),
            P("pool", None, "head", None),
            P("head", None, None),
            P("head", None, None),
            P("head", "pool"),
        ),
        out_specs=P("head", None, "pool"),
        check_vma=False,
    )
```

time: 385 us -> 146 us (0.38)
  waiting for transfers between devices: 260 us -> 0 us
  Pallas kernels: 0 us -> 132 us
  matrix products: 50.3 us -> 0 us
  local copies, waits for them, and re-layouts: 30.3 us -> 7.87 us
  between operations: 13.6 us -> 0.13 us
  other arithmetic: 17.3 us -> 6.06 us
  starting transfers between devices: 10.5 us -> 0 us
    pallas_call x0 -> x2, Pallas kernels: none -> 132 us  [the longest x1 88.2 us: attend(): pl.pallas_call(attend_kernel, out_shape=(jax.ShapeDtypeStruct((64, 2048),...]
    all_to_all x1 -> x0, waiting for transfers between devices: 114 us -> none  [per_device(): lax.all_to_all(packed, 'pool', split_axis=0, concat_axis=0, tiled=True)]
    reduce_scatter x1 -> x0, waiting for transfers between devices: 77.1 us -> none  [per_device(): lax.psum_scatter(partial_value, 'head', scatter_dimension=0, tiled=True)]
    all_gather x1 -> x0, waiting for transfers between devices: 68.6 us -> none  [per_device(): lax.all_gather(heads_out, 'pool', axis=0, tiled=True)]
    dot_general x8 -> x0, matrix products: 50.3 us -> none  [the longest x1 20.9 us: per_device(): jnp.einsum('rthc,rlc->rthl', query_full, cached, preferred_element_type=j...]
    gather x1 -> x0, local copies, waits for them, and re-layouts: 22.9 us -> none  [per_device(): cached = page_pool[block_table].reshape(rows_dev, -1, lat_width)]
    all_to_all x1 -> x0, starting transfers between devices: 10.4 us -> none  [per_device(): lax.all_to_all(packed, 'pool', split_axis=0, concat_axis=0, tiled=True)]
    concatenate x2, other arithmetic: 8.54 us -> 1.2 us  [the longest x1 1.12 us: attend(): q3 = jnp.concatenate([q, none, none, q[:, 128:]], axis=1)]
  transfers between devices with their start and end apart: 3 -> 0, of which waited for: 3 -> 0; matrix products, arithmetic and copies ran while one was open for 1% -> 0% of each run, Pallas kernels for 0% -> 0%
where the time goes in v1:
time: 146 us
  Pallas kernels  132 us (90%)
  local copies, waits for them, and re-layouts  7.87 us (5%)
  other arithmetic  6.06 us (4%)
    pallas_call x1, Pallas kernels, attend(): pl.pallas_call(attend_kernel, out_shape=(jax.ShapeDtypeStruct((64, 2048),...  88.2 us
    pallas_call x1, Pallas kernels, project(): pl.pallas_call(project_kernel, out_shape=jax.ShapeDtypeStruct((4, 64, 224...  44 us

profile of v1, /device:TPU:17, one launch (start us, length us, event | category | flops | bytes accessed | tf_op | source)
XLA Modules:
  0.0 146.2 jit_solution(16569510037973336857)
XLA Ops:
  0.0 0.1 stack.43
  0.1 0.8 compare_reduce_fusion
  1.0 0.1 pad.3.clone
  1.0 0.9 fusion.1
  2.0 0.7 and_select_fusion
  2.6 0.1 copy.26
  2.7 0.1 copy.25
  2.8 0.1 copy.27
  2.9 0.7 pad_add_fusion.pick
  3.5 0.1 iota_compare_fusion.1
  3.6 0.1 add.230
  3.7 0.1 iota.81
  3.8 0.1 iota.82
  3.9 0.1 iota_add_fusion
  4.0 0.1 add.226
  4.1 0.1 iota.89
  4.2 0.1 fusion
  4.2 0.1 iota.91
  4.4 0.1 pad_add_fusion.1
  4.4 1.0 convert_reduce_fusion.1
  5.4 1.6 %reshape.133.fresh = bf16[64,576]{1,0:T(8,128)(2,1)} reshape(bf16[16,4,576]{2,1,0:T(4,128)(2,1)} %param.15) | data formatting | bytes 147456 | tf_op jit(solution)/shard_map/reshape | solution.py:461
  7.0 1.3 copy.28
  8.3 0.0 copy-start
  8.4 1.1 pad_maximum_fusion.q3
  9.5 0.5 log_multiply_fusion
  10.0 1.0 reshape.138.bias
  11.1 0.0 copy-done
  11.1 1.3 copy.29.w_out
  12.4 88.2 %handoff_attend.1 = (bf16[64,2048]{1,0:T(8,128)(2,1)}, bf16[3,2048,224]{2,1,0:T(8,128)(2,1)}) custom-call(s32[8,3]{1,0:T(8,128)} %pad_add_fusion.pick, bf16[1024,384]{1,0:T(8,128)(2,1)} %pad_maximum_fusion.q3, f32[16,7168]{1,0:T(8,128)} %reshape.138.bias, bf16[32,64,576]{2,1,0:T(8,128)(2,1)} %span.1, bf16[3072,576]{1,0:T(8,128)(2,1)} %bitcast.21, ...), custom_call_target="tpu_custom_call" | custom-call | tf_op jit(solution)/shard_map/handoff_attend/pallas_call | solution.py:433
  100.6 44.0 %gather_project.1 = bf16[4,64,224]{2,1,0:T(8,128)(2,1)} custom-call(bf16[64,2048]{1,0:T(8,128)(2,1)} %get-tuple-element.7.heads, bf16[2048,224]{1,0:T(8,128)(2,1)} %copy.29.w_out, bf16[3,2048,224]{2,1,0:T(8,128)(2,1)} %get-tuple-element.8.wall), custom_call_target="tpu_custom_call" | custom-call | tf_op jit(solution)/shard_map/gather_project/pallas_call | solution.py:465
  144.6 1.6 %copy.31 = bf16[4,16,4,224]{3,2,1,0:T(4,128)(2,1)} copy(bf16[4,16,4,224]{3,1,2,0:T(8,128)(2,1)} %bitcast.24) | data formatting | bytes 229376 | tf_op jit(solution)/shard_map/transpose | solution.py:482
  (15 shorter events, 0.1 us)
Async XLA Ops:
  8.3 2.8 %copy-start = (bf16[2048,224]{0,1:T(8,128)(2,1)S(1)}, bf16[2048,224]{0,1:T(8,128)(2,1)}, u32[]{:S(2)}) copy-start(bf16[2048,224]{0,1:T(8,128)(2,1)} %param.19) | copy-start | bytes 2752516

commit v2 on v1

v2 whole, which is shorter than its diff:
```python
import functools

import jax
import jax.numpy as jnp
from jax import lax
from jax.experimental import pallas as pl
from jax.experimental.pallas import tpu as pltpu
from jax.sharding import PartitionSpec as P

MESH = pl.DeviceIdType.MESH
F32 = jnp.float32
BF16 = jnp.bfloat16
NT = (((1,), (1,)), ((), ()))
QT = 1024
SENT = (8, 9, 10, 0, 1, 2, 3, 4, 5, 6, 7)


def coords():
    p = lax.axis_index("pool")
    h = lax.axis_index("head")
    return p // 4, lax.rem(p // 2, 2), lax.rem(p, 2), h // 2, lax.rem(h, 2)


DIRECT = ((0, 0), (0, 1), (0, 2), (0, 3), (1, 0), (1, 1), (7, 0), (7, 1))


def split_offset(i, y, xh):
    dz0 = jnp.where(i == 0, 1 + 6 * (y // 2), jnp.where(i == 1, 3, 5))
    k0 = jnp.where(i == 0, 2 + lax.rem(y, 2), lax.rem(y + i, 4))
    dz1 = jnp.where(i == 0, 2, jnp.where(i == 1, 6, 4))
    k1 = lax.rem(y + i, 4)
    return jnp.where(xh == 0, dz0, dz1), jnp.where(xh == 0, k0, k1)


def offset_of(j, y, xh):
    return DIRECT[j] if j < 8 else split_offset(j - 8, y, xh)


def peer_of(j, z, xl, c, y, xh, sign):
    dz, k = offset_of(j, y, xh)
    return lax.rem(z + 8 + sign * dz, 8) * 4 + lax.rem(xl + k // 2, 2) * 2 + lax.rem(c + k, 2)


def attend_kernel(
    pick, q3, bias, span, resident, fresh, w_uk, w_uv, w_out,
    heads_out, wall,
    span_v, res_v, uk_v, uv_v, fresh_v, bias_v, sendbuf, near, arr, q_main, q_low, q_high, turned, acc, m_s, l_s, out_v,
    load_sem, res_sem, zsend, zrecv, xsend, xrecv, ysend, yrecv, wsend, wrecv, out_sem,
):
    z, xl, c, y, xh = coords()
    p = lax.axis_index("pool")
    h = lax.axis_index("head")
    g = lax.rem(p, 4)
    up = lax.rem(y + 1, 4) * 2 + xh
    down = lax.rem(y + 3, 4) * 2 + xh
    across = y * 2 + 1 - xh
    core_mate = p + 1 - 2 * c
    xl_mate = p + 2 - 4 * xl

    loads = [
        pltpu.make_async_copy(span, span_v, load_sem.at[0]),
        pltpu.make_async_copy(w_uk, uk_v, load_sem.at[1]),
        pltpu.make_async_copy(fresh, fresh_v, load_sem.at[2]),
        pltpu.make_async_copy(w_uv, uv_v, load_sem.at[3]),
    ]
    res_loads = [
        pltpu.make_async_copy(resident.at[pl.ds(512 * n, 512)], res_v.at[pl.ds(512 * n, 512)], res_sem.at[n])
        for n in range(6)
    ]
    bias_load = pltpu.make_async_copy(bias, bias_v, load_sem.at[4])
    loads[0].start()

    barrier = pltpu.get_barrier_semaphore()

    def greet(pool_to, head_to):
        pl.semaphore_signal(barrier, inc=1, device_id=(pool_to, head_to), device_id_type=MESH)

    for j in range(1, 11):
        for sign in (1, -1):
            greet(peer_of(j, z, xl, c, y, xh, sign), h)
    greet(p, up)
    greet(p, down)
    greet(core_mate, h)
    greet(xl_mate, h)
    greet(p, across)

    loads[0].wait()
    for one in loads[1:3] + res_loads[:2] + [bias_load] + res_loads[2:] + loads[3:]:
        one.start()
    zcopies = {}
    for j in SENT:
        live = pick[0, j] >= 0
        for ab in range(2):
            at = jnp.maximum(pick[0, j], 0) if ab else 31 - jnp.maximum(pick[1, j], 0)
            block = span_v[at] * live.astype(F32).astype(BF16)
            for slab in range(4):
                sendbuf[j, ab * 4 + slab] = block[:, slab * 128 : (slab + 1) * 128]
            if ab == 0:
                low = block[:, 512:]
            else:
                sendbuf[j, 8] = jnp.concatenate([low, block[:, 512:]], axis=1)
        landing = near.at[j // 4, :, j % 4] if j < 8 else arr.at[0, :, j - 8]
        if j == 0:
            keep = pltpu.make_async_copy(sendbuf.at[0], landing, zrecv.at[0])
            keep.start()
            continue
        zcopies[j] = pltpu.make_async_remote_copy(
            src_ref=sendbuf.at[j], dst_ref=landing, send_sem=zsend.at[j], recv_sem=zrecv.at[j],
            device_id=(peer_of(j, z, xl, c, y, xh, 1), h), device_id_type=MESH,
        )
        if j == 10:
            pl.semaphore_wait(barrier, 25)
            for one in (8, 9, 10):
                zcopies[one].start()
        if j in (1, 2, 3):
            zcopies[j].start()

    def wcopy(src, owner, to, n):
        slot = lax.rem(owner - lax.rem(to, 4) + 4, 4) - 1
        return pltpu.make_async_remote_copy(
            src_ref=src, dst_ref=wall.at[slot], send_sem=wsend.at[n], recv_sem=wrecv.at[n],
            device_id=(to, h), device_id_type=MESH,
        )

    w_mate = wcopy(w_out, g, core_mate, 0)
    w_far = wcopy(w_out, g, xl_mate, 1)
    w_pass = wcopy(wall.at[1], lax.rem(g + 2, 4), core_mate, 2)
    loads[1].wait()

    @pl.loop(0, 8)
    def _(two):
        cols = pl.ds(pl.multiple_of(two * 128, 128), 128)
        both = []
        for n in range(2):
            at = pl.ds(pl.multiple_of(two * 128 + n * 64, 64), 64)
            both.append(jnp.dot(q3[at, :128], uk_v[two * 2 + n], preferred_element_type=F32))
        q_main[:, cols] = jnp.concatenate(both, axis=0).astype(BF16).T
        rope = q3[cols, 128:192].T
        none = jnp.zeros((64, 128), BF16)
        q_low[:, cols] = jnp.concatenate([rope, none], axis=0)
        q_high[:, cols] = jnp.concatenate([none, rope], axis=0)

    scale = 1.4426950408889634 * 192 ** -0.5

    def fold(cols, s, values, first=False):
        top = jnp.max(s, axis=0, keepdims=True)
        if not first:
            before = m_s[:1, cols]
            top = jnp.maximum(top, before)
        p_ = jnp.exp2(s - top)
        total = jnp.sum(p_, axis=0, keepdims=True)
        mix = jnp.dot(values, p_.astype(BF16), preferred_element_type=F32)
        if not first:
            fade = jnp.exp2(before - top)
            total = total + l_s[:1, cols] * fade
            mix = mix + acc[:, cols] * fade
        acc[:, cols] = mix
        m_s[:1, cols] = top
        l_s[:1, cols] = total

    def each_tile(body):
        for t in range(1024 // QT):
            body(pl.ds(t * QT, QT))

    loads[2].wait()
    new = fresh_v[...].reshape(64, 576)
    turned[:, :64] = new[:, :512].T

    def fresh_tile(cols):
        s = jnp.dot(new[:, :512], q_main[:, cols], preferred_element_type=F32)
        s = s + jnp.dot(new[:, 512:], q_low[:64, cols], preferred_element_type=F32)
        token = lax.broadcasted_iota(jnp.int32, s.shape, 0)
        lane = lax.broadcasted_iota(jnp.int32, s.shape, 1)
        seen = ((lane & 15) == (token >> 2)) & (((lane >> 4) & 3) >= (token & 3))
        fold(cols, jnp.where(seen, s * scale, -jnp.inf), turned[:, :64], first=True)

    each_tile(fresh_tile)

    def biased(s, toks):
        b = bias_v[toks, :]
        return s * scale + jnp.concatenate([b] * (QT // 128), axis=1)

    def resident_chunk(n):
        res_loads[n].wait()
        toks = pl.ds(512 * n, 512)
        turned[:, :512] = res_v[toks, :512].T

        def tile(cols):
            s = jnp.dot(res_v[toks, :512], q_main[:, cols], preferred_element_type=F32)
            s = s + jnp.dot(res_v[toks, 512:], q_low[:64, cols], preferred_element_type=F32)
            fold(cols, biased(s, toks), turned[:, :512])

        each_tile(tile)

    def arrived_chunk(held, first, count):
        half = 64 * count
        for ab in range(2):
            for j in range(4):
                turned[j * 128 : (j + 1) * 128, ab * half : (ab + 1) * half] = (
                    held[ab * 4 + j].reshape(half, 128).T
                )

        def tile(cols):
            rope = held[8].reshape(half, 128)
            main = jnp.concatenate(
                [
                    jnp.concatenate([held[ab * 4 + j].reshape(half, 128) for j in range(4)], axis=1)
                    for ab in range(2)
                ],
                axis=0,
            )
            s = jnp.dot(main, q_main[:, cols], preferred_element_type=F32)
            s = s + jnp.concatenate(
                [jnp.dot(rope, q[:, cols], preferred_element_type=F32) for q in (q_low, q_high)], axis=0
            )
            fold(cols, biased(s, pl.ds(first, 2 * half)), turned[:, : 2 * half])

        each_tile(tile)

    def near_chunk(n):
        arrived_chunk(near.at[n], 3072 + 512 * n, 4)

    def far_chunk(rel):
        arrived_chunk(arr.at[rel], 4096 + 768 * rel, 6)

    def ycopy(i, way, kind):
        landing = 2 if kind else (3 if way == 0 else 1)
        source = 0 if kind == 0 else (3 if way == 0 else 1)
        return pltpu.make_async_remote_copy(
            src_ref=arr.at[source, :, i], dst_ref=arr.at[landing, :, i],
            send_sem=ysend.at[way, kind, i], recv_sem=yrecv.at[way, kind, i],
            device_id=(p, up if way == 0 else down), device_id_type=MESH,
        )

    def xcopy(i):
        return pltpu.make_async_remote_copy(
            src_ref=arr.at[0, :, i], dst_ref=arr.at[0, :, 3 + i],
            send_sem=xsend.at[i], recv_sem=xrecv.at[i], device_id=(p, across), device_id_type=MESH,
        )

    def own_step(i):
        if i < 3:
            zcopies[8 + i].wait_recv()
            xcopy(i).start()
        else:
            xcopy(i - 3).wait_recv()
        ycopy(i, 0, 0).start()
        ycopy(i, 1, 0).start()

    def pass_step(i):
        ycopy(i, 0, 0).wait_recv()
        ycopy(i, 1, 0).wait_recv()
        ycopy(i, i % 2, 1).start()

    bias_load.wait()
    resident_chunk(0)
    own_step(0)
    resident_chunk(1)
    resident_chunk(2)
    own_step(1)
    own_step(2)
    for j in (8, 9, 10):
        zcopies[j].wait_send()
    for j in (4, 5, 6, 7):
        zcopies[j].start()
    own_step(3)
    pass_step(0)
    resident_chunk(3)
    own_step(4)
    own_step(5)
    w_mate.start()
    w_far.start()
    resident_chunk(4)
    pass_step(1)
    pass_step(2)
    resident_chunk(5)
    keep.wait()
    for j in (1, 2, 3):
        zcopies[j].wait_recv()
    pass_step(3)
    near_chunk(0)
    pass_step(4)
    pass_step(5)
    far_chunk(0)
    far_chunk(3)
    far_chunk(1)
    for j in (4, 5, 6, 7):
        zcopies[j].wait_recv()
    near_chunk(1)
    w_far.wait_recv()
    w_pass.start()
    for i in range(6):
        ycopy(i, i % 2, 1).wait_recv()
    far_chunk(2)

    loads[3].wait()

    @pl.loop(0, 8)
    def _(two):
        cols = pl.ds(pl.multiple_of(two * 128, 128), 128)
        mixed = (acc[:, cols] / l_s[:1, cols]).astype(BF16).T
        for n in range(2):
            out_v[:, pl.ds(pl.multiple_of(two * 256 + n * 128, 128), 128)] = jnp.dot(
                mixed[n * 64 : (n + 1) * 64], uv_v[two * 2 + n], preferred_element_type=F32
            ).astype(BF16)

    done = pltpu.make_async_copy(out_v, heads_out, out_sem)
    done.start()

    for j in range(1, 8):
        zcopies[j].wait_send()
    for i in range(3):
        xcopy(i).wait_send()
    for i in range(6):
        ycopy(i, 0, 0).wait_send()
        ycopy(i, 1, 0).wait_send()
        ycopy(i, i % 2, 1).wait_send()
    w_mate.wait()
    w_far.wait_send()
    w_pass.wait()
    done.wait()


def project_kernel(
    heads, w_out, wall,
    out,
    w_v, hbuf, tiles, landed, load_sem, zsend, zrecv, rsend, rrecv,
):
    p = lax.axis_index("pool")
    h = lax.axis_index("head")
    z, g = p // 4, lax.rem(p, 4)
    right = lax.rem(z + 1, 8) * 4 + g
    left = lax.rem(z + 7, 8) * 4 + g

    own = pltpu.make_async_copy(heads, hbuf.at[0], load_sem.at[4])
    own.start()
    w_loads = [pltpu.make_async_copy(w_out, w_v.at[0], load_sem.at[0])] + [
        pltpu.make_async_copy(wall.at[i], w_v.at[i + 1], load_sem.at[i + 1]) for i in range(3)
    ]
    for one in w_loads:
        one.start()

    barrier = pltpu.get_barrier_semaphore()

    def greet(pool_to, head_to):
        pl.semaphore_signal(barrier, inc=1, device_id=(pool_to, head_to), device_id_type=MESH)

    greet(right, h)
    greet(left, h)
    for dh in range(8):
        for i in range(4):
            if dh or i:
                greet(z * 4 + lax.rem(g + i, 4), lax.rem(h + dh, 8))
    pl.semaphore_wait(barrier, 33)

    def zcopy(way, a, half):
        rows = pl.ds(32 * half, 32)
        src = 0 if a == 1 else 2 * (a - 1) - 1 + way
        dst = 7 if a == 4 else 2 * a - 1 + way
        return pltpu.make_async_remote_copy(
            src_ref=hbuf.at[src, rows], dst_ref=hbuf.at[dst, rows],
            send_sem=zsend.at[way, a - 1, half], recv_sem=zrecv.at[way, a - 1, half],
            device_id=(right if way == 0 else left, h), device_id_type=MESH,
        )

    own.wait()
    order = [(0, 0), (0, 1), (1, 1), (1, 0)]
    for way, half in order:
        zcopy(way, 1, half).start()

    def tile_copy(slot, i, to_head):
        return pltpu.make_async_remote_copy(
            src_ref=tiles.at[slot, i], dst_ref=landed.at[h, g],
            send_sem=rsend.at[slot, i], recv_sem=rrecv.at[h, g],
            device_id=(z * 4 + lax.rem(g + i, 4), to_head), device_id_type=MESH,
        )

    def slot_head(slot):
        if slot == 0:
            return z
        if slot == 7:
            return lax.rem(z + 4, 8)
        a = (slot + 1) // 2
        return lax.rem(z + 8 - a, 8) if slot % 2 else lax.rem(z + a, 8)

    def multiply(first, count):
        lhs = hbuf[pl.ds(first, count)].reshape(64 * count, 2048)
        for i in range(4):
            part = lax.dot_general(lhs, w_v[i], NT, preferred_element_type=F32).astype(BF16)
            for n in range(count):
                slot = first + n
                to_head = slot_head(slot)
                tiles[slot, i] = part[64 * n : 64 * (n + 1)]
                copy = tile_copy(slot, i, to_head)
                if i == 0:
                    @pl.when(to_head != h)
                    def _(copy=copy):
                        copy.start()

                    @pl.when(to_head == h)
                    def _(slot=slot):
                        landed[h, g] = tiles[slot, 0]
                else:
                    copy.start()

    for one in w_loads:
        one.wait()
    multiply(0, 1)
    for a in range(1, 4):
        for way, half in order:
            zcopy(way, a, half).wait_recv()
            if a < 3 or way == half:
                zcopy(way, a + 1, half).start()
        multiply(2 * a - 1, 2)
    zcopy(0, 4, 0).wait_recv()
    zcopy(1, 4, 1).wait_recv()
    multiply(7, 1)

    for dh in range(8):
        for i in range(4):
            if dh or i:
                hh, gg = lax.rem(h + dh, 8), lax.rem(g + i, 4)
                pltpu.make_async_remote_copy(
                    src_ref=tiles.at[0, 0], dst_ref=landed.at[hh, gg],
                    send_sem=rsend.at[0, 0], recv_sem=rrecv.at[hh, gg],
                    device_id=(z * 4 + gg, hh), device_id_type=MESH,
                ).wait_recv()
    total = landed[0].astype(F32)
    for n in range(1, 8):
        total = total + landed[n].astype(F32)
    out[...] = total.astype(BF16)

    for way, half in order:
        for a in range(1, 5):
            if a < 4 or way == half:
                zcopy(way, a, half).wait_send()
    for slot in range(8):
        to_head = slot_head(slot)
        for i in range(4):
            if i == 0:
                @pl.when(to_head != h)
                def _(slot=slot, to_head=to_head):
                    tile_copy(slot, 0, to_head).wait_send()
            else:
                tile_copy(slot, i, to_head).wait_send()


ANY = pl.BlockSpec(memory_space=pl.ANY)
VMEM = pl.BlockSpec(memory_space=pltpu.VMEM)
SMEM = pl.BlockSpec(memory_space=pltpu.SMEM)
DMA = pltpu.SemaphoreType.DMA


def attend(span_cache, destination, resident, block_table, lengths, new_latent, query, w_uk, w_uv, w_out):
    z, xl, c, y, xh = coords()
    near = jnp.array(DIRECT, jnp.int32)
    dz, k = split_offset(jnp.arange(3, dtype=jnp.int32), y, xh)
    dz, k = jnp.concatenate([near[:, 0], dz]), jnp.concatenate([near[:, 1], k])
    owners = lax.rem(z + dz, 8) * 4 + lax.rem(xl + k // 2, 2) * 2 + lax.rem(c + k, 2)
    at = jnp.arange(32, dtype=jnp.int32)
    places = jnp.stack([at, 31 - at])[:, None, :]
    pick = jnp.max(jnp.where(destination[:, 0] == owners[:, None], places, -1), axis=2)

    member = lax.rem(y + jnp.arange(4, dtype=jnp.int32)[:, None], 4)
    m = jnp.arange(6, dtype=jnp.int32)[None, :]
    far_dz, far_k = split_offset(lax.rem(m, 3), member, lax.rem(xh + m // 3, 2))

    def slots(dz, k):
        source = lax.rem(z + 8 - dz, 8) * 4 + lax.rem(xl + k // 2, 2) * 2 + lax.rem(c + k, 2)
        return (48 + 2 * source[:, None, :] + jnp.arange(2, dtype=jnp.int32)[None, :, None]).reshape(-1)

    pages = jnp.concatenate([
        jnp.arange(48, dtype=jnp.int32),
        slots(near[:, 0].reshape(2, 4), near[:, 1].reshape(2, 4)),
        slots(far_dz, far_k),
    ])
    table = jnp.tile(block_table.T, (1, 8))
    length = jnp.tile(lengths, 8)
    hit = table[None, :, :] == pages[:, None, None]
    col = jnp.arange(32, dtype=jnp.int32)[None, :, None]
    full = (length // 64)[None, None, :]
    count = jnp.sum((hit & (col < full)).astype(F32), axis=1)
    partial = jnp.sum((hit & (col == full)).astype(F32), axis=1)
    inside = jnp.arange(64, dtype=jnp.int32)[:, None] < lax.rem(length, 64)[None, :]
    reads = count[:, None, :] + jnp.where(inside[None], partial[:, None, :], 0.0)
    bias = jnp.log2(reads).reshape(112 * 64, 128)

    q3 = query.transpose(2, 1, 0, 3).reshape(1024, 192)

    return pl.pallas_call(
        attend_kernel,
        out_shape=(
            jax.ShapeDtypeStruct((64, 2048), BF16),
            jax.ShapeDtypeStruct((3, 224, 2048), BF16),
        ),
        in_specs=[SMEM, VMEM, ANY, ANY, ANY, ANY, ANY, ANY, ANY],
        out_specs=(ANY, ANY),
        scratch_shapes=[
            pltpu.VMEM((32, 64, 576), BF16),
            pltpu.VMEM((3072, 576), BF16),
            pltpu.VMEM((16, 128, 512), BF16),
            pltpu.VMEM((16, 512, 128), BF16),
            pltpu.VMEM((16, 4, 576), BF16),
            pltpu.VMEM((7168, 128), F32),
            pltpu.VMEM((11, 9, 64, 128), BF16),
            pltpu.VMEM((2, 9, 4, 64, 128), BF16),
            pltpu.VMEM((4, 9, 6, 64, 128), BF16),
            pltpu.VMEM((512, 1024), BF16),
            pltpu.VMEM((128, 1024), BF16),
            pltpu.VMEM((128, 1024), BF16),
            pltpu.VMEM((512, 768), BF16),
            pltpu.VMEM((512, 1024), F32),
            pltpu.VMEM((8, 1024), F32),
            pltpu.VMEM((8, 1024), F32),
            pltpu.VMEM((64, 2048), BF16),
            DMA((5,)), DMA((6,)), DMA((11,)), DMA((11,)), DMA((3,)), DMA((3,)),
            DMA((2, 2, 6)), DMA((2, 2, 6)), DMA((3,)), DMA((3,)), DMA,
        ],
        compiler_params=pltpu.CompilerParams(
            collective_id=0, has_side_effects=True, vmem_limit_bytes=56 * 1024 * 1024
        ),
        name="handoff_attend",
    )(pick, q3, bias, span_cache, resident.reshape(3072, 576), new_latent, w_uk, w_uv, w_out)


def project(heads, w_out, wall):
    out = pl.pallas_call(
        project_kernel,
        out_shape=jax.ShapeDtypeStruct((4, 64, 224), BF16),
        in_specs=[ANY, ANY, ANY],
        out_specs=VMEM,
        scratch_shapes=[
            pltpu.VMEM((4, 224, 2048), BF16),
            pltpu.VMEM((8, 64, 2048), BF16),
            pltpu.VMEM((8, 4, 64, 224), BF16),
            pltpu.VMEM((8, 4, 64, 224), BF16),
            DMA((5,)), DMA((2, 4, 2)), DMA((2, 4, 2)), DMA((8, 4)), DMA((8, 4)),
        ],
        compiler_params=pltpu.CompilerParams(
            collective_id=1, has_side_effects=True, vmem_limit_bytes=56 * 1024 * 1024
        ),
        name="gather_project",
    )(heads, w_out, wall)
    return out.reshape(4, 4, 16, 224).transpose(0, 2, 1, 3).reshape(64, 4, 224)


def per_device(
    span_cache, destination, resident, block_table, lengths, new_latent, query, w_uk, w_uv, w_out
):
    w_out = w_out.T
    heads, wall = attend(
        span_cache, destination, resident, block_table, lengths, new_latent, query, w_uk, w_uv, w_out
    )
    return project(heads, w_out, wall)


def solution(mesh):
    return jax.shard_map(
        per_device,
        mesh=mesh,
        in_specs=(
            P("pool", None, None),
            P("pool", None),
            P("pool", None, None),
            P("pool", None),
            P("pool"),
            P("pool", None, None),
            P("pool", None, "head", None),
            P("head", None, None),
            P("head", None, None),
            P("head", "pool"),
        ),
        out_specs=P("head", None, "pool"),
        check_vma=False,
    )
```

time: 146 us -> 117 us (0.80)
  Pallas kernels: 132 us -> 104 us
  local copies, waits for them, and re-layouts: 7.87 us -> 6.19 us
    pallas_call x1, Pallas kernels: 88.2 us -> 60.5 us  [attend(): pl.pallas_call(attend_kernel, out_shape=(jax.ShapeDtypeStruct((64, 2048),...]
    reshape x1 -> x0, local copies, waits for them, and re-layouts: 1.57 us -> none  [attend(): new_latent.reshape(64, 576)]
    add x4 -> x6, other arithmetic: 0.1 us -> 1.59 us  [the longest x4 0.81 us: slots(): 48 + 2 * source[:, None, :] + jnp.arange(2, dtype=jnp.int32)[None, :, None]]
where the time goes in v2:
time: 117 us
  Pallas kernels  104 us (89%)
  other arithmetic  6.84 us (6%)
  local copies, waits for them, and re-layouts  6.19 us (5%)
    pallas_call x1, Pallas kernels, attend(): pl.pallas_call(attend_kernel, out_shape=(jax.ShapeDtypeStruct((64, 2048),...  60.5 us
    pallas_call x1, Pallas kernels, project(): pl.pallas_call(project_kernel, out_shape=jax.ShapeDtypeStruct((4, 64, 224...  43.4 us
    another operation x1, other arithmetic, attend(): bias = jnp.log2(reads).reshape(112 * 64, 128)  2.64 us

profile of v2, /device:TPU:17, one launch (start us, length us, event | category | flops | bytes accessed | tf_op | source)
XLA Modules:
  0.0 117.0 jit_solution(4357030429337980276)
XLA Ops:
  0.0 0.8 fusion.26
  0.8 0.7 add_reduce_fusion
  1.5 0.1 sub.84
  1.5 0.7 fusion.16
  2.4 0.1 add.323
  2.5 0.1 multiply_add_fusion
  2.6 0.7 broadcast_compare_fusion
  3.3 0.1 add.343
  3.4 0.1 pad_add_fusion.2
  3.5 0.7 tile.19
  4.1 0.1 tile.20
  4.2 0.3 select_reduce_fusion
  4.5 0.6 copy.20.pick
  5.2 0.7 tile.8
  5.9 0.1 copy.19
  5.9 0.7 convert_reduce_fusion.1
  6.7 2.1 %copy.18 = bf16[16,4,16,192]{3,2,1,0:T(8,128)(2,1)} copy(bf16[16,4,16,192]{3,0,1,2:T(8,128)(2,1)} %bitcast.18) | data formatting | bytes 786432 | tf_op jit(solution)/shard_map/transpose | solution.py:488
  8.8 2.6 %log_multiply_fusion = f32[112,64,128]{2,1,0:T(8,128)} fusion(f32[112,128]{1,0:T(8,128)S(1)} %get-tuple-element.10, f32[112,128]{1,0:T(8,128)S(1)} %get-tuple-element.9, pred[64,128]{1,0:T(8,128)(4,1)S(1)} %iota_compare_fusion), kind=kLoop, calls=%fused_computation | loop fusion | flops 2752512 | bytes 3792896 | tf_op jit(solution)/shard_map/log2 | solution.py:486
  11.5 60.5 %handoff_attend.1 = (bf16[64,2048]{1,0:T(8,128)(2,1)}, bf16[3,224,2048]{2,1,0:T(8,128)(2,1)}) custom-call(s32[2,11]{1,0:T(2,128)} %copy.20.pick, bf16[1024,192]{1,0:T(8,128)(2,1)} %bitcast.16, f32[7168,128]{1,0:T(8,128)} %bitcast.12, bf16[32,64,576]{2,1,0:T(8,128)(2,1)} %span.1, bf16[3072,576]{1,0:T(8,128)(2,1)} %bitcast.13, bf16[16,4,576]{2,1,0:T(4,128)(2,1)} %fresh.1, ...), custom_call_target="tpu_custom_call" | custom-call | tf_op jit(solution)/shard_map/handoff_attend/pallas_call | solution.py:490
  72.0 43.4 %gather_project.1 = bf16[4,64,224]{2,1,0:T(8,128)(2,1)} custom-call(bf16[64,2048]{1,0:T(8,128)(2,1)} %get-tuple-element.7.heads, bf16[224,2048]{1,0:T(8,128)(2,1)} %bitcast.15, bf16[3,224,2048]{2,1,0:T(8,128)(2,1)} %get-tuple-element.8.wall), custom_call_target="tpu_custom_call" | custom-call | tf_op jit(solution)/shard_map/gather_project/pallas_call | solution.py:527
  115.4 1.6 %copy.21 = bf16[4,16,4,224]{3,2,1,0:T(4,128)(2,1)} copy(bf16[4,16,4,224]{3,1,2,0:T(8,128)(2,1)} %bitcast.17) | data formatting | bytes 229376 | tf_op jit(solution)/shard_map/transpose | solution.py:544
  (15 shorter events, 0.1 us)

commit v3 on v2

v3 whole, which is shorter than its diff:
```python
import functools

import jax
import jax.numpy as jnp
from jax import lax
from jax.experimental import pallas as pl
from jax.experimental.pallas import tpu as pltpu
from jax.sharding import PartitionSpec as P

MESH = pl.DeviceIdType.MESH
F32 = jnp.float32
BF16 = jnp.bfloat16
NT = (((1,), (1,)), ((), ()))
QT = 1024
SENT = (8, 9, 10, 0, 1, 2, 3, 4, 5, 6, 7)


def coords():
    p = lax.axis_index("pool")
    h = lax.axis_index("head")
    return p // 4, lax.rem(p // 2, 2), lax.rem(p, 2), h // 2, lax.rem(h, 2)


DIRECT = ((0, 0), (0, 1), (0, 2), (0, 3), (1, 0), (1, 1), (7, 0), (7, 1))


def split_offset(i, y, xh):
    dz0, k0 = (1 + 6 * (y // 2), 2 + lax.rem(y, 2)) if i == 0 else (2 * i + 1, lax.rem(y + i, 4))
    dz1, k1 = (2, 6, 4)[i], lax.rem(y + i, 4)
    return jnp.where(xh == 0, dz0, dz1), jnp.where(xh == 0, k0, k1)


def offset_of(j, y, xh):
    return DIRECT[j] if j < 8 else split_offset(j - 8, y, xh)


def peer_of(j, z, xl, c, y, xh, sign):
    dz, k = offset_of(j, y, xh)
    return pool_at(dz, k, z, xl, c, sign)


def pool_at(dz, k, z, xl, c, sign):
    return lax.rem(z + 8 + sign * dz, 8) * 4 + lax.rem(xl + k // 2, 2) * 2 + lax.rem(c + k, 2)


def kernel(
    dest, table, query, span, resident, fresh, w_uk, w_uv, w_out,
    out,
    span_v, res_v, uk_v, uv_v, fresh_v, query_v, query_f, bias_v, sendbuf, near, arr, q_main, q_low, q_high, turned,
    acc, m_s, l_s, w_v, hbuf, tiles, landed,
    load_sem, res_sem, zsend, zrecv, xsend, xrecv, ysend, yrecv, wsend, wrecv, hsend, hrecv, rsend, rrecv,
):
    z, xl, c, y, xh = coords()
    p = lax.axis_index("pool")
    h = lax.axis_index("head")
    g = lax.rem(p, 4)
    up = lax.rem(y + 1, 4) * 2 + xh
    down = lax.rem(y + 3, 4) * 2 + xh
    across = y * 2 + 1 - xh
    core_mate = p + 1 - 2 * c
    xl_mate = p + 2 - 4 * xl
    right = lax.rem(z + 1, 8) * 4 + g
    left = lax.rem(z + 7, 8) * 4 + g

    load = lambda src, dst, n: pltpu.make_async_copy(src, dst, load_sem.at[n])
    span_load = load(span, span_v, 0)
    query_load = load(query, query_v, 1)
    uk_load = load(w_uk, uk_v, 2)
    fresh_load = load(fresh, fresh_v, 3)
    uv_load = load(w_uv, uv_v, 4)
    w_load = load(w_out, w_v.at[0], 5)
    res_loads = [
        pltpu.make_async_copy(resident.at[pl.ds(512 * n, 512)], res_v.at[pl.ds(512 * n, 512)], res_sem.at[n])
        for n in range(6)
    ]
    span_load.start()

    barrier = pltpu.get_barrier_semaphore()

    def greet(pool_to, head_to):
        pl.semaphore_signal(barrier, inc=1, device_id=(pool_to, head_to), device_id_type=MESH)

    for j in range(1, 11):
        for sign in (1, -1):
            greet(peer_of(j, z, xl, c, y, xh, sign), h)
    greet(p, up)
    greet(p, down)
    greet(p, across)
    greet(core_mate, h)
    greet(xl_mate, h)
    greet(right, h)
    greet(left, h)
    for dh in range(8):
        for i in range(4):
            if dh or i:
                greet(z * 4 + lax.rem(g + i, 4), lax.rem(h + dh, 8))

    owners = [peer_of(j, z, xl, c, y, xh, 1) for j in range(11)]
    last = [jnp.int32(-1)] * 11
    first = [jnp.int32(-1)] * 11
    for b in range(32):
        ahead, behind = dest[b, 0], dest[31 - b, 0]
        for j in range(11):
            last[j] = jnp.where(ahead == owners[j], b, last[j])
            first[j] = jnp.where(behind == owners[j], 31 - b, first[j])

    span_load.wait()
    for one in [query_load, uk_load, fresh_load] + res_loads + [uv_load, w_load]:
        one.start()
    zcopies = {}
    for j in SENT:
        live = (last[j] >= 0).astype(F32).astype(BF16)
        for ab in range(2):
            block = span_v[jnp.maximum(last[j] if ab else first[j], 0)] * live
            for slab in range(4):
                sendbuf[j, ab * 4 + slab] = block[:, slab * 128 : (slab + 1) * 128]
            if ab == 0:
                low = block[:, 512:]
            else:
                sendbuf[j, 8] = jnp.concatenate([low, block[:, 512:]], axis=1)
        if j == 0:
            keep = pltpu.make_async_copy(sendbuf.at[0], near.at[0, :, 0], zrecv.at[0])
            keep.start()
            continue
        zcopies[j] = pltpu.make_async_remote_copy(
            src_ref=sendbuf.at[j],
            dst_ref=near.at[j // 4, :, j % 4] if j < 8 else arr.at[0, :, j - 8],
            send_sem=zsend.at[j],
            recv_sem=zrecv.at[j],
            device_id=(peer_of(j, z, xl, c, y, xh, 1), h), device_id_type=MESH,
        )
        if j == 8:
            pl.semaphore_wait(barrier, 58)
        if j in (8, 9, 10, 1, 2, 3):
            zcopies[j].start()

    def wcopy(src, owner, to, n):
        slot = lax.rem(owner - lax.rem(to, 4) + 4, 4)
        return pltpu.make_async_remote_copy(
            src_ref=src, dst_ref=w_v.at[slot], send_sem=wsend.at[n], recv_sem=wrecv.at[n],
            device_id=(to, h), device_id_type=MESH,
        )

    w_mate = wcopy(w_out, g, core_mate, 0)
    w_far = wcopy(w_out, g, xl_mate, 1)
    w_pass = wcopy(w_v.at[2], lax.rem(g + 2, 4), core_mate, 2)

    query_load.wait()
    query_f[0] = query_v[:, :128].astype(F32)
    query_f[1] = jnp.concatenate([query_v[:, 128:].astype(F32), jnp.zeros((1024, 64), F32)], axis=1)
    uk_load.wait()

    @pl.loop(0, 8)
    def _(two):
        cols = pl.ds(pl.multiple_of(two * 128, 128), 128)
        plain, rope = (
            jnp.concatenate([query_f[part, pl.ds(two * 2 + n, 64, stride=16), :] for n in range(2)], axis=0).astype(BF16)
            for part in range(2)
        )
        q_main[:, cols] = jnp.concatenate(
            [
                jnp.dot(plain[64 * n : 64 * (n + 1)], uk_v[two * 2 + n], preferred_element_type=F32)
                for n in range(2)
            ],
            axis=0,
        ).astype(BF16).T
        rope = rope.T
        q_low[:, cols] = rope
        q_high[:, cols] = jnp.concatenate([rope[64:], rope[:64]], axis=0)

    scale = 1.4426950408889634 * 192 ** -0.5

    def fold(cols, s, values, first=False):
        top = jnp.max(s, axis=0, keepdims=True)
        if not first:
            before = m_s[:1, cols]
            top = jnp.maximum(top, before)
        p_ = jnp.exp2(s - top)
        total = jnp.sum(p_, axis=0, keepdims=True)
        mix = jnp.dot(values, p_.astype(BF16), preferred_element_type=F32)
        if not first:
            fade = jnp.exp2(before - top)
            total = total + l_s[:1, cols] * fade
            mix = mix + acc[:, cols] * fade
        acc[:, cols] = mix
        m_s[:1, cols] = top
        l_s[:1, cols] = total

    fresh_load.wait()
    new = fresh_v[...].reshape(64, 576)
    turned[:, :64] = new[:, :512].T
    ALL = pl.ds(0, 1024)
    s = jnp.dot(new[:, :512], q_main[...], preferred_element_type=F32)
    s = s + jnp.dot(new[:, 512:], q_low[:64, :], preferred_element_type=F32)
    token = lax.broadcasted_iota(jnp.int32, s.shape, 0)
    lane = lax.broadcasted_iota(jnp.int32, s.shape, 1)
    seen = (((lane >> 2) & 15) == (token >> 2)) & ((lane & 3) >= (token & 3))
    fold(ALL, jnp.where(seen, s * scale, -jnp.inf), turned[:, :64], first=True)

    length = table[32:33, :]
    whole = length >> 6
    position = lax.broadcasted_iota(jnp.int32, (32, 128), 0)
    full = jnp.where(position < whole, table[:32, :], -1)
    partial = jnp.max(jnp.where(position == whole, table[:32, :], -1), axis=0, keepdims=True)
    inside = lax.broadcasted_iota(jnp.int32, (64, 128), 0) < (length & 63)

    def fill_bias(n, page):
        count = jnp.sum(jnp.where(full == page, 1.0, 0.0), axis=0, keepdims=True)
        reads = count + jnp.where(inside & (partial == page), 1.0, 0.0)
        bias_v[64 * n : 64 * (n + 1), :] = jnp.where(reads > 0, jnp.log2(jnp.maximum(reads, 1.0)), -jnp.inf)

    def fill_pairs(n, offsets):
        for ab in range(2):
            for m, (dz, k) in enumerate(offsets):
                fill_bias(n + ab * len(offsets) + m, 48 + 2 * pool_at(dz, k, z, xl, c, -1) + ab)

    def biased(s, toks, width):
        b = bias_v[toks, :]
        return s * scale + jnp.concatenate([b] * (width // 128), axis=1)

    def resident_chunk(n):
        for page in range(8 * n, 8 * n + 8):
            fill_bias(page, page)
        res_loads[n].wait()
        toks = pl.ds(512 * n, 512)
        turned[:, :512] = res_v[toks, :512].T
        s = jnp.dot(res_v[toks, :512], q_main[...], preferred_element_type=F32)
        s = s + jnp.dot(res_v[toks, 512:], q_low[:64, :], preferred_element_type=F32)
        fold(ALL, biased(s, toks, 1024), turned[:, :512])

    def arrived_chunk(held, first, count, tiles_of=(ALL,), after=None):
        half = 64 * count
        for ab in range(2):
            for j in range(4):
                turned[j * 128 : (j + 1) * 128, ab * half : (ab + 1) * half] = (
                    held[ab * 4 + j].reshape(half, 128).T
                )
        for cols in tiles_of:
            rope = held[8].reshape(half, 128)
            main = jnp.concatenate(
                [
                    jnp.concatenate([held[ab * 4 + j].reshape(half, 128) for j in range(4)], axis=1)
                    for ab in range(2)
                ],
                axis=0,
            )
            s = jnp.dot(main, q_main[:, cols], preferred_element_type=F32)
            s = s + jnp.concatenate(
                [jnp.dot(rope, q[:, cols], preferred_element_type=F32) for q in (q_low, q_high)], axis=0
            )
            fold(cols, biased(s, pl.ds(first, 2 * half), cols.size), turned[:, : 2 * half])
            if after is not None:
                after(cols)

    def near_chunk(n):
        fill_pairs(48 + 8 * n, DIRECT[4 * n : 4 * n + 4])
        arrived_chunk(near.at[n], 3072 + 512 * n, 4)

    def far_bias(rel):
        member = lax.rem(y + rel, 4)
        fill_pairs(64 + 12 * rel, [split_offset(m % 3, member, lax.rem(xh + m // 3, 2)) for m in range(6)])

    def far_chunk(rel, **how):
        arrived_chunk(arr.at[rel], 4096 + 768 * rel, 6, **how)

    def xcopy(i):
        return pltpu.make_async_remote_copy(
            src_ref=arr.at[0, :, i], dst_ref=arr.at[0, :, 3 + i],
            send_sem=xsend.at[i], recv_sem=xrecv.at[i], device_id=(p, across), device_id_type=MESH,
        )

    def ycopy(n, way, kind):
        landing = 2 if kind else (3 if way == 0 else 1)
        source = 0 if kind == 0 else (3 if way == 0 else 1)
        return pltpu.make_async_remote_copy(
            src_ref=arr.at[source, :, n], dst_ref=arr.at[landing, :, n],
            send_sem=ysend.at[way, kind, n], recv_sem=yrecv.at[way, kind, n],
            device_id=(p, up if way == 0 else down), device_id_type=MESH,
        )

    def own_step(n):
        if n < 3:
            zcopies[8 + n].wait_recv()
            xcopy(n).start()
        else:
            xcopy(n - 3).wait_recv()
        ycopy(n, 0, 0).start()
        ycopy(n, 1, 0).start()

    def pass_step(n):
        ycopy(n, 0, 0).wait_recv()
        ycopy(n, 1, 0).wait_recv()
        ycopy(n, n % 2, 1).start()

    resident_chunk(0)
    own_step(0)
    resident_chunk(1)
    own_step(1)
    own_step(2)
    for j in (8, 9, 10):
        zcopies[j].wait_send()
    for j in (4, 5, 6, 7):
        zcopies[j].start()
    own_step(3)
    pass_step(0)
    own_step(4)
    own_step(5)
    w_mate.start()
    w_far.start()
    pass_step(1)
    pass_step(2)
    resident_chunk(2)
    pass_step(3)
    pass_step(4)
    pass_step(5)
    resident_chunk(3)
    resident_chunk(4)
    resident_chunk(5)
    keep.wait()
    for j in (1, 2, 3):
        zcopies[j].wait_recv()
    near_chunk(0)
    for rel in range(4):
        far_bias(rel)
    far_chunk(0)
    for j in (4, 5, 6, 7):
        zcopies[j].wait_recv()
    near_chunk(1)
    far_chunk(3)
    far_chunk(1)
    for n in range(6):
        ycopy(n, n % 2, 1).wait_recv()
    uv_load.wait()

    def hcopy(way, a, half):
        cols = pl.ds(1024 * half, 1024)
        src = 0 if a == 1 else 2 * (a - 1) - 1 + way
        dst = 7 if a == 4 else 2 * a - 1 + way
        return pltpu.make_async_remote_copy(
            src_ref=hbuf.at[src, :, cols], dst_ref=hbuf.at[dst, :, cols],
            send_sem=hsend.at[way, a - 1, half], recv_sem=hrecv.at[way, a - 1, half],
            device_id=(right if way == 0 else left, h), device_id_type=MESH,
        )

    def finish(cols):
        for two in range(cols.start // 128, (cols.start + cols.size) // 128):
            at = pl.ds(two * 128, 128)
            mixed = (acc[:, at] / l_s[:1, at]).astype(BF16).T
            for n in range(2):
                hbuf[0, :, two * 256 + n * 128 : two * 256 + (n + 1) * 128] = jnp.dot(
                    mixed[n * 64 : (n + 1) * 64], uv_v[two * 2 + n], preferred_element_type=F32
                ).astype(BF16)
        half = cols.start // 512
        hcopy(0, 1, half).start()
        hcopy(1, 1, half).start()

    far_chunk(2, tiles_of=(pl.ds(0, 512), pl.ds(512, 512)), after=finish)

    def tile_copy(slot, i, to_head):
        return pltpu.make_async_remote_copy(
            src_ref=tiles.at[slot, i], dst_ref=landed.at[h, g],
            send_sem=rsend.at[slot, i], recv_sem=rrecv.at[h, g],
            device_id=(z * 4 + lax.rem(g + i, 4), to_head), device_id_type=MESH,
        )

    def slot_head(slot):
        if slot == 0:
            return z
        if slot == 7:
            return lax.rem(z + 4, 8)
        a = (slot + 1) // 2
        return lax.rem(z + 8 - a, 8) if slot % 2 else lax.rem(z + a, 8)

    def multiply(first, count):
        lhs = hbuf[pl.ds(first, count)].reshape(64 * count, 2048)
        for i in range(4):
            part = lax.dot_general(lhs, w_v[i], NT, preferred_element_type=F32).astype(BF16)
            for n in range(count):
                slot = first + n
                to_head = slot_head(slot)
                tiles[slot, i] = part[64 * n : 64 * (n + 1)]
                copy = tile_copy(slot, i, to_head)
                if i == 0:
                    @pl.when(to_head != h)
                    def _(copy=copy):
                        copy.start()

                    @pl.when(to_head == h)
                    def _(slot=slot):
                        landed[h, g] = tiles[slot, 0]
                else:
                    copy.start()

    w_far.wait_recv()
    w_pass.start()
    w_load.wait()
    w_mate.wait_recv()
    w_pass.wait_recv()
    multiply(0, 1)
    order = [(0, 0), (1, 0), (0, 1), (1, 1)]
    for a in range(1, 4):
        for way, half in order:
            hcopy(way, a, half).wait_recv()
            if a < 3 or way == half:
                hcopy(way, a + 1, half).start()
        multiply(2 * a - 1, 2)
    hcopy(0, 4, 0).wait_recv()
    hcopy(1, 4, 1).wait_recv()
    multiply(7, 1)

    for dh in range(8):
        for i in range(4):
            if dh or i:
                hh, gg = lax.rem(h + dh, 8), lax.rem(g + i, 4)
                pltpu.make_async_remote_copy(
                    src_ref=tiles.at[0, 0], dst_ref=landed.at[hh, gg],
                    send_sem=rsend.at[0, 0], recv_sem=rrecv.at[hh, gg],
                    device_id=(z * 4 + gg, hh), device_id_type=MESH,
                ).wait_recv()
    total = landed[0].astype(F32)
    for n in range(1, 8):
        total = total + landed[n].astype(F32)
    out[...] = total.astype(BF16)

    for j in range(1, 8):
        zcopies[j].wait_send()
    for i in range(3):
        xcopy(i).wait_send()
    for n in range(6):
        ycopy(n, 0, 0).wait_send()
        ycopy(n, 1, 0).wait_send()
        ycopy(n, n % 2, 1).wait_send()
    w_mate.wait_send()
    w_far.wait_send()
    w_pass.wait_send()
    for way, half in order:
        for a in range(1, 5):
            if a < 4 or way == half:
                hcopy(way, a, half).wait_send()
    for slot in range(8):
        to_head = slot_head(slot)
        for i in range(4):
            if i == 0:
                @pl.when(to_head != h)
                def _(slot=slot, to_head=to_head):
                    tile_copy(slot, 0, to_head).wait_send()
            else:
                tile_copy(slot, i, to_head).wait_send()


ANY = pl.BlockSpec(memory_space=pl.ANY)
VMEM = pl.BlockSpec(memory_space=pltpu.VMEM)
SMEM = pl.BlockSpec(memory_space=pltpu.SMEM)
DMA = pltpu.SemaphoreType.DMA


def per_device(
    span_cache, destination, resident, block_table, lengths, new_latent, query, w_uk, w_uv, w_out
):
    table = jnp.concatenate([block_table.T, lengths[None, :], jnp.zeros((7, 16), jnp.int32)], axis=0)
    table = jnp.broadcast_to(table[:, None, :, None], (40, 2, 16, 4)).reshape(40, 128)
    out = pl.pallas_call(
        kernel,
        out_shape=jax.ShapeDtypeStruct((4, 64, 224), BF16),
        in_specs=[SMEM, VMEM] + [ANY] * 7,
        out_specs=VMEM,
        scratch_shapes=[
            pltpu.VMEM((32, 64, 576), BF16),
            pltpu.VMEM((3072, 576), BF16),
            pltpu.VMEM((16, 128, 512), BF16),
            pltpu.VMEM((16, 512, 128), BF16),
            pltpu.VMEM((16, 4, 576), BF16),
            pltpu.VMEM((1024, 192), BF16),
            pltpu.VMEM((2, 1024, 128), F32),
            pltpu.VMEM((7168, 128), F32),
            pltpu.VMEM((11, 9, 64, 128), BF16),
            pltpu.VMEM((2, 9, 4, 64, 128), BF16),
            pltpu.VMEM((4, 9, 6, 64, 128), BF16),
            pltpu.VMEM((512, 1024), BF16),
            pltpu.VMEM((128, 1024), BF16),
            pltpu.VMEM((128, 1024), BF16),
            pltpu.VMEM((512, 768), BF16),
            pltpu.VMEM((512, 1024), F32),
            pltpu.VMEM((8, 1024), F32),
            pltpu.VMEM((8, 1024), F32),
            pltpu.VMEM((4, 224, 2048), BF16),
            pltpu.VMEM((8, 64, 2048), BF16),
            pltpu.VMEM((8, 4, 64, 224), BF16),
            pltpu.VMEM((8, 4, 64, 224), BF16),
            DMA((6,)), DMA((6,)), DMA((11,)), DMA((11,)), DMA((3,)), DMA((3,)),
            DMA((2, 2, 6)), DMA((2, 2, 6)), DMA((3,)), DMA((3,)),
            DMA((2, 4, 2)), DMA((2, 4, 2)), DMA((8, 4)), DMA((8, 4)),
        ],
        compiler_params=pltpu.CompilerParams(
            collective_id=0, has_side_effects=True, vmem_limit_bytes=60 * 1024 * 1024
        ),
        name="handoff_attend_project",
    )(
        destination, table, query.reshape(1024, 192), span_cache, resident.reshape(3072, 576), new_latent,
        w_uk, w_uv, w_out.T,
    )
    return out.reshape(64, 4, 224)


def solution(mesh):
    return jax.shard_map(
        per_device,
        mesh=mesh,
        in_specs=(
            P("pool", None, None),
            P("pool", None),
            P("pool", None, None),
            P("pool", None),
            P("pool"),
            P("pool", None, None),
            P("pool", None, "head", None),
            P("head", None, None),
            P("head", None, None),
            P("head", "pool"),
        ),
        out_specs=P("head", None, "pool"),
        check_vma=False,
    )
```

time: 117 us -> 110 us (0.940)
  other arithmetic: 6.84 us -> 0.77 us
  local copies, waits for them, and re-layouts: 6.19 us -> 4.44 us
    transpose x2 -> x0, local copies, waits for them, and re-layouts: 3.78 us -> none  [the longest x1 2.15 us: attend(): q3 = query.transpose(2, 1, 0, 3).reshape(1024, 192)]
    another operation x2 -> x0, other arithmetic: 2.65 us -> none  [the longest x1 2.64 us: attend(): bias = jnp.log2(reads).reshape(112 * 64, 128)]
    reshape x0 -> x2, local copies, waits for them, and re-layouts: none -> 2.29 us  [the longest x1 1.61 us: per_device(): return out.reshape(64, 4, 224)]
    add x6 -> x0, other arithmetic: 1.59 us -> none  [the longest x4 0.81 us: slots(): 48 + 2 * source[:, None, :] + jnp.arange(2, dtype=jnp.int32)[None, :, None]]
    another operation x4 -> x0, local copies, waits for them, and re-layouts: 1.5 us -> none  [the longest x2 0.76 us: attend(): table = jnp.tile(block_table.T, (1, 8))]
    unnamed x0 -> x1, local copies, waits for them, and re-layouts: none -> 1.33 us
    pallas_call x2 -> x1, Pallas kernels: 104 us -> 104 us  [per_device(): pl.pallas_call(kernel, out_shape=jax.ShapeDtypeStruct((4, 64, 224), BF16)...]
where the time goes in v3:
time: 110 us; the launch traced here: 109 us
  Pallas kernels  104 us (95%)
  local copies, waits for them, and re-layouts  4.44 us (4%)
    pallas_call x1, Pallas kernels, per_device(): pl.pallas_call(kernel, out_shape=jax.ShapeDtypeStruct((4, 64, 224), BF16)...  104 us

profile of v3, /device:TPU:17, one launch (start us, length us, event | category | flops | bytes accessed | tf_op | source)
XLA Modules:
  0.0 109.4 jit_solution(890270521594440945)
XLA Ops:
  0.0 0.1 pad.2.clone
  0.1 0.7 copy.14
  0.8 0.8 add_add_fusion
  1.6 1.3 %copy.15.dest = s32[32,1]{1,0:T(8,128)} copy(s32[32,1]{0,1:T(1,128)} %param.11) | data formatting | bytes 256 | tf_op args[1]
  2.9 0.7 copy.16.table
  3.6 104.2 %handoff_attend_project.1 = bf16[4,64,224]{2,1,0:T(8,128)(2,1)} custom-call(s32[32,1]{1,0:T(8,128)} %copy.15.dest, s32[40,128]{1,0:T(8,128)} %copy.16.table, bf16[1024,192]{1,0:T(8,128)(2,1)} %bitcast.8, bf16[32,64,576]{2,1,0:T(8,128)(2,1)} %span.1, bf16[3072,576]{1,0:T(8,128)(2,1)} %bitcast.6, bf16[16,4,576]{2,1,0:T(4,128)(2,1)} %fresh.1, ...), custom_call_target="tpu_custom_call" | custom-call | tf_op jit(solution)/shard_map/handoff_attend_project/pallas_call | solution.py:462
  107.8 1.6 %reshape.16 = bf16[64,4,224]{2,1,0:T(4,128)(2,1)} reshape(bf16[4,64,224]{2,1,0:T(8,128)(2,1)} %handoff_attend_project.1) | data formatting | bytes 229376 | tf_op jit(solution)/shard_map/reshape | solution.py:502
  (2 shorter events, 0.0 us)

commit v4 on v3

--- a/solution.py
+++ b/solution.py
@@ -131,7 +131,7 @@
         )
         if j == 8:
             pl.semaphore_wait(barrier, 58)
-        if j in (8, 9, 10, 1, 2, 3):
+        if j in (8, 1, 2, 3):
             zcopies[j].start()
 
     def wcopy(src, owner, to, n):
@@ -292,34 +292,34 @@
         ycopy(n, 1, 0).wait_recv()
         ycopy(n, n % 2, 1).start()
 
+    zcopies[9].start()
+    zcopies[10].start()
     resident_chunk(0)
     own_step(0)
     resident_chunk(1)
     own_step(1)
     own_step(2)
-    for j in (8, 9, 10):
-        zcopies[j].wait_send()
     for j in (4, 5, 6, 7):
         zcopies[j].start()
+    w_mate.start()
+    w_far.start()
     own_step(3)
     pass_step(0)
     own_step(4)
     own_step(5)
-    w_mate.start()
-    w_far.start()
     pass_step(1)
+    resident_chunk(2)
     pass_step(2)
-    resident_chunk(2)
+    resident_chunk(3)
     pass_step(3)
+    resident_chunk(4)
     pass_step(4)
-    pass_step(5)
-    resident_chunk(3)
-    resident_chunk(4)
     resident_chunk(5)
     keep.wait()
     for j in (1, 2, 3):
         zcopies[j].wait_recv()
     near_chunk(0)
+    pass_step(5)
     for rel in range(4):
         far_bias(rel)
     far_chunk(0)
@@ -328,6 +328,8 @@
     near_chunk(1)
     far_chunk(3)
     far_chunk(1)
+    w_far.wait_recv()
+    w_pass.start()
     for n in range(6):
         ycopy(n, n % 2, 1).wait_recv()
     uv_load.wait()
@@ -391,19 +393,19 @@
                 else:
                     copy.start()
 
-    w_far.wait_recv()
-    w_pass.start()
-    w_load.wait()
-    w_mate.wait_recv()
-    w_pass.wait_recv()
-    multiply(0, 1)
     order = [(0, 0), (1, 0), (0, 1), (1, 1)]
     for a in range(1, 4):
         for way, half in order:
             hcopy(way, a, half).wait_recv()
             if a < 3 or way == half:
                 hcopy(way, a + 1, half).start()
-        multiply(2 * a - 1, 2)
+        if a == 1:
+            w_load.wait()
+            w_mate.wait_recv()
+            w_pass.wait_recv()
+            multiply(0, 3)
+        else:
+            multiply(2 * a - 1, 2)
     hcopy(0, 4, 0).wait_recv()
     hcopy(1, 4, 1).wait_recv()
     multiply(7, 1)
@@ -422,7 +424,7 @@
         total = total + landed[n].astype(F32)
     out[...] = total.astype(BF16)
 
-    for j in range(1, 8):
+    for j in range(1, 11):
         zcopies[j].wait_send()
     for i in range(3):
         xcopy(i).wait_send()

time: 110 us -> 102 us (0.927)
  Pallas kernels: 104 us -> 96 us
    pallas_call x1, Pallas kernels: 104 us -> 96 us  [per_device(): pl.pallas_call(kernel, out_shape=jax.ShapeDtypeStruct((4, 64, 224), BF16)...]
where the time goes in v4:
time: 102 us; the launch traced here: 101 us
  Pallas kernels  96 us (94%)
  local copies, waits for them, and re-layouts  4.44 us (4%)
    pallas_call x1, Pallas kernels, per_device(): pl.pallas_call(kernel, out_shape=jax.ShapeDtypeStruct((4, 64, 224), BF16)...  96 us

profile of v4, /device:TPU:17, one launch (start us, length us, event | category | flops | bytes accessed | tf_op | source)
XLA Modules:
  0.0 101.2 jit_solution(6218001249742103697)
XLA Ops:
  0.0 0.1 pad.2.clone
  0.1 0.7 copy.14
  0.8 0.8 add_add_fusion
  1.6 1.3 %copy.15.dest = s32[32,1]{1,0:T(8,128)} copy(s32[32,1]{0,1:T(1,128)} %param.11) | data formatting | bytes 256 | tf_op args[1]
  2.9 0.7 copy.16.table
  3.6 96.0 %handoff_attend_project.1 = bf16[4,64,224]{2,1,0:T(8,128)(2,1)} custom-call(s32[32,1]{1,0:T(8,128)} %copy.15.dest, s32[40,128]{1,0:T(8,128)} %copy.16.table, bf16[1024,192]{1,0:T(8,128)(2,1)} %bitcast.8, bf16[32,64,576]{2,1,0:T(8,128)(2,1)} %span.1, bf16[3072,576]{1,0:T(8,128)(2,1)} %bitcast.6, bf16[16,4,576]{2,1,0:T(4,128)(2,1)} %fresh.1, ...), custom_call_target="tpu_custom_call" | custom-call | tf_op jit(solution)/shard_map/handoff_attend_project/pallas_call | solution.py:464
  99.6 1.6 %reshape.16 = bf16[64,4,224]{2,1,0:T(4,128)(2,1)} reshape(bf16[4,64,224]{2,1,0:T(8,128)(2,1)} %handoff_attend_project.1) | data formatting | bytes 229376 | tf_op jit(solution)/shard_map/reshape | solution.py:504
  (2 shorter events, 0.0 us)

commit v5 on v4

--- a/solution.py
+++ b/solution.py
@@ -44,9 +44,9 @@
 
 
 def kernel(
-    dest, table, query, span, resident, fresh, w_uk, w_uv, w_out,
+    given, query, span, resident, fresh, w_uk, w_uv, w_out,
     out,
-    span_v, res_v, uk_v, uv_v, fresh_v, query_v, query_f, bias_v, sendbuf, near, arr, q_main, q_low, q_high, turned,
+    dest, table, span_v, res_v, uk_v, uv_v, fresh_v, query_v, query_f, bias_v, sendbuf, near, arr, q_main, q_low, q_high, turned,
     acc, m_s, l_s, w_v, hbuf, tiles, landed,
     load_sem, res_sem, zsend, zrecv, xsend, xrecv, ysend, yrecv, wsend, wrecv, hsend, hrecv, rsend, rrecv,
 ):
@@ -73,7 +73,11 @@
         pltpu.make_async_copy(resident.at[pl.ds(512 * n, 512)], res_v.at[pl.ds(512 * n, 512)], res_sem.at[n])
         for n in range(6)
     ]
+    table_load = load(given, table, 6)
+    dest_load = load(given.at[pl.ds(32, 8)], dest, 7)
+    dest_load.start()
     span_load.start()
+    table_load.start()
 
     barrier = pltpu.get_barrier_semaphore()
 
@@ -97,9 +101,10 @@
 
     owners = [peer_of(j, z, xl, c, y, xh, 1) for j in range(11)]
     last = [jnp.int32(-1)] * 11
+    dest_load.wait()
     first = [jnp.int32(-1)] * 11
     for b in range(32):
-        ahead, behind = dest[b, 0], dest[31 - b, 0]
+        ahead, behind = dest[1, b], dest[1, 31 - b]
         for j in range(11):
             last[j] = jnp.where(ahead == owners[j], b, last[j])
             first[j] = jnp.where(behind == owners[j], 31 - b, first[j])
@@ -197,6 +202,7 @@
     seen = (((lane >> 2) & 15) == (token >> 2)) & ((lane & 3) >= (token & 3))
     fold(ALL, jnp.where(seen, s * scale, -jnp.inf), turned[:, :64], first=True)
 
+    table_load.wait()
     length = table[32:33, :]
     whole = length >> 6
     position = lax.broadcasted_iota(jnp.int32, (32, 128), 0)
@@ -459,14 +465,18 @@
 def per_device(
     span_cache, destination, resident, block_table, lengths, new_latent, query, w_uk, w_uv, w_out
 ):
-    table = jnp.concatenate([block_table.T, lengths[None, :], jnp.zeros((7, 16), jnp.int32)], axis=0)
-    table = jnp.broadcast_to(table[:, None, :, None], (40, 2, 16, 4)).reshape(40, 128)
+    table = jnp.concatenate([block_table.T, lengths[None, :]], axis=0)
+    table = jnp.broadcast_to(table[:, None, :, None], (33, 2, 16, 4)).reshape(33, 128)
+    owners = jnp.pad(destination.reshape(1, 32), ((0, 6), (0, 96)))
+    given = jnp.concatenate([table, owners], axis=0)
     out = pl.pallas_call(
         kernel,
         out_shape=jax.ShapeDtypeStruct((4, 64, 224), BF16),
-        in_specs=[SMEM, VMEM] + [ANY] * 7,
+        in_specs=[ANY] * 8,
         out_specs=VMEM,
         scratch_shapes=[
+            pltpu.SMEM((8, 128), jnp.int32),
+            pltpu.VMEM((40, 128), jnp.int32),
             pltpu.VMEM((32, 64, 576), BF16),
             pltpu.VMEM((3072, 576), BF16),
             pltpu.VMEM((16, 128, 512), BF16),
@@ -489,7 +499,7 @@
             pltpu.VMEM((8, 64, 2048), BF16),
             pltpu.VMEM((8, 4, 64, 224), BF16),
             pltpu.VMEM((8, 4, 64, 224), BF16),
-            DMA((6,)), DMA((6,)), DMA((11,)), DMA((11,)), DMA((3,)), DMA((3,)),
+            DMA((8,)), DMA((6,)), DMA((11,)), DMA((11,)), DMA((3,)), DMA((3,)),
             DMA((2, 2, 6)), DMA((2, 2, 6)), DMA((3,)), DMA((3,)),
             DMA((2, 4, 2)), DMA((2, 4, 2)), DMA((8, 4)), DMA((8, 4)),
         ],
@@ -498,7 +508,7 @@
         ),
         name="handoff_attend_project",
     )(
-        destination, table, query.reshape(1024, 192), span_cache, resident.reshape(3072, 576), new_latent,
+        given, query.reshape(1024, 192), span_cache, resident.reshape(3072, 576), new_latent,
         w_uk, w_uv, w_out.T,
     )
     return out.reshape(64, 4, 224)

time: 102 us -> 99.7 us (0.977)
  local copies, waits for them, and re-layouts: 4.44 us -> 2.41 us
  other arithmetic: 0.77 us -> 2.06 us
    unnamed x1 -> x0, local copies, waits for them, and re-layouts: 1.33 us -> none
    concatenate x1 -> x2, other arithmetic: 0.77 us -> 2.06 us  [the longest x1 1.29 us: per_device(): given = jnp.concatenate([table, owners], axis=0)]
where the time goes in v5:
time: 99.7 us; the launch traced here: 99.5 us
  Pallas kernels  95 us (95%)
  local copies, waits for them, and re-layouts  2.41 us (2%)
  other arithmetic  2.06 us (2%)
    pallas_call x1, Pallas kernels, per_device(): pl.pallas_call(kernel, out_shape=jax.ShapeDtypeStruct((4, 64, 224), BF16)...  95 us

profile of v5, /device:TPU:17, one launch (start us, length us, event | category | flops | bytes accessed | tf_op | source)
XLA Modules:
  0.0 99.5 jit_solution(2381637289673800084)
XLA Ops:
  0.0 0.7 copy.13
  0.7 0.8 pad_add_fusion.1
  1.5 0.1 copy.14
  1.6 1.3 %pad_add_fusion.given = s32[40,128]{1,0:T(8,128)} fusion(s32[1,32]{1,0:T(1,128)} %bitcast.13, s32[33,128]{1,0:T(8,128)S(1)} %copy.14), kind=kLoop, calls=%fused_computation | loop fusion | flops 5120 | bytes 37504 | tf_op jit(solution)/shard_map/concatenate | solution.py:471
  2.9 95.0 %handoff_attend_project.1 = bf16[4,64,224]{2,1,0:T(8,128)(2,1)} custom-call(s32[40,128]{1,0:T(8,128)} %pad_add_fusion.given, bf16[1024,192]{1,0:T(8,128)(2,1)} %bitcast.9, bf16[32,64,576]{2,1,0:T(8,128)(2,1)} %span.1, bf16[3072,576]{1,0:T(8,128)(2,1)} %bitcast.7, bf16[16,4,576]{2,1,0:T(4,128)(2,1)} %fresh.1, bf16[16,128,512]{2,1,0:T(8,128)(2,1)} %w_uk.1, ...), custom_call_target="tpu_custom_call" | custom-call | tf_op jit(solution)/shard_map/handoff_attend_project/pallas_call | solution.py:472
  97.9 1.6 %reshape.20 = bf16[64,4,224]{2,1,0:T(4,128)(2,1)} reshape(bf16[4,64,224]{2,1,0:T(8,128)(2,1)} %handoff_attend_project.1) | data formatting | bytes 229376 | tf_op jit(solution)/shard_map/reshape | solution.py:514
  (1 shorter events, 0.0 us)

commit v6 on v5

--- a/solution.py
+++ b/solution.py
@@ -150,9 +150,10 @@
     w_far = wcopy(w_out, g, xl_mate, 1)
     w_pass = wcopy(w_v.at[2], lax.rem(g + 2, 4), core_mate, 2)
 
+    scale = 1.4426950408889634 * 192 ** -0.5
     query_load.wait()
     query_f[0] = query_v[:, :128].astype(F32)
-    query_f[1] = jnp.concatenate([query_v[:, 128:].astype(F32), jnp.zeros((1024, 64), F32)], axis=1)
+    query_f[1] = jnp.concatenate([query_v[:, 128:].astype(F32) * scale, jnp.zeros((1024, 64), F32)], axis=1)
     uk_load.wait()
 
     @pl.loop(0, 8)
@@ -162,18 +163,16 @@
             jnp.concatenate([query_f[part, pl.ds(two * 2 + n, 64, stride=16), :] for n in range(2)], axis=0).astype(BF16)
             for part in range(2)
         )
-        q_main[:, cols] = jnp.concatenate(
+        q_main[:, cols] = (scale * jnp.concatenate(
             [
                 jnp.dot(plain[64 * n : 64 * (n + 1)], uk_v[two * 2 + n], preferred_element_type=F32)
                 for n in range(2)
             ],
             axis=0,
-        ).astype(BF16).T
+        )).astype(BF16).T
         rope = rope.T
         q_low[:, cols] = rope
         q_high[:, cols] = jnp.concatenate([rope[64:], rope[:64]], axis=0)
-
-    scale = 1.4426950408889634 * 192 ** -0.5
 
     def fold(cols, s, values, first=False):
         top = jnp.max(s, axis=0, keepdims=True)
@@ -200,7 +199,7 @@
     token = lax.broadcasted_iota(jnp.int32, s.shape, 0)
     lane = lax.broadcasted_iota(jnp.int32, s.shape, 1)
     seen = (((lane >> 2) & 15) == (token >> 2)) & ((lane & 3) >= (token & 3))
-    fold(ALL, jnp.where(seen, s * scale, -jnp.inf), turned[:, :64], first=True)
+    fold(ALL, jnp.where(seen, s, -jnp.inf), turned[:, :64], first=True)
 
     table_load.wait()
     length = table[32:33, :]
@@ -222,7 +221,7 @@
 
     def biased(s, toks, width):
         b = bias_v[toks, :]
-        return s * scale + jnp.concatenate([b] * (width // 128), axis=1)
+        return s + jnp.concatenate([b] * (width // 128), axis=1)
 
     def resident_chunk(n):
         for page in range(8 * n, 8 * n + 8):

time: 99.7 us -> 99.4 us (level)
  no operation moved by 1% of the time
where the time goes in v6:
time: 99.4 us; the launch traced here: 99.2 us
  Pallas kernels  94.7 us (95%)
  local copies, waits for them, and re-layouts  2.41 us (2%)
  other arithmetic  2.06 us (2%)
    pallas_call x1, Pallas kernels, per_device(): pl.pallas_call(kernel, out_shape=jax.ShapeDtypeStruct((4, 64, 224), BF16)...  94.7 us

profile of v6, /device:TPU:17, one launch (start us, length us, event | category | flops | bytes accessed | tf_op | source)
XLA Modules:
  0.0 99.2 jit_solution(17141759815046909045)
XLA Ops:
  0.0 0.7 copy.13
  0.7 0.8 pad_add_fusion.1
  1.5 0.1 copy.14
  1.6 1.3 %pad_add_fusion.given = s32[40,128]{1,0:T(8,128)} fusion(s32[1,32]{1,0:T(1,128)} %bitcast.13, s32[33,128]{1,0:T(8,128)S(1)} %copy.14), kind=kLoop, calls=%fused_computation | loop fusion | flops 5120 | bytes 37504 | tf_op jit(solution)/shard_map/concatenate | solution.py:470
  2.9 94.7 %handoff_attend_project.1 = bf16[4,64,224]{2,1,0:T(8,128)(2,1)} custom-call(s32[40,128]{1,0:T(8,128)} %pad_add_fusion.given, bf16[1024,192]{1,0:T(8,128)(2,1)} %bitcast.9, bf16[32,64,576]{2,1,0:T(8,128)(2,1)} %span.1, bf16[3072,576]{1,0:T(8,128)(2,1)} %bitcast.7, bf16[16,4,576]{2,1,0:T(4,128)(2,1)} %fresh.1, bf16[16,128,512]{2,1,0:T(8,128)(2,1)} %w_uk.1, ...), custom_call_target="tpu_custom_call" | custom-call | tf_op jit(solution)/shard_map/handoff_attend_project/pallas_call | solution.py:471
  97.6 1.6 %reshape.20 = bf16[64,4,224]{2,1,0:T(4,128)(2,1)} reshape(bf16[4,64,224]{2,1,0:T(8,128)(2,1)} %handoff_attend_project.1) | data formatting | bytes 229376 | tf_op jit(solution)/shard_map/reshape | solution.py:513
  (1 shorter events, 0.0 us)
